TPU v7x, 32 devices: a whole 2x2x4 slice. The times are simulated.
32 devices in a mesh: day: 4 (over y, x), tile: 8 (over z, core).
Axes of the slice: x: 2, y: 2, z: 4, core: 2. Of those that a mesh axis runs over, the one named last changes fastest.
Arguments:
- scene_rows: bfloat16 [4, 4, 8, 512, 128], P(None, 'day', 'tile'), may hold values from -6 to 6
- granule_list: int32 [32, 8, 4, 3], P('day', 'tile'), may hold values from 0 to 16, as said below
- land_mask: int32 [64, 1024], P('day', 'tile'), may hold values 0 or 1
- in_weight: bfloat16 [16, 4], replicated, may hold values from -3 to 3
- obs_bias: float32 [16], replicated, may hold values from -3 to 3
- time_taps: float32 [4, 16, 3], replicated, may hold values from -3 to 3
- mix_weight: bfloat16 [4, 16, 16], replicated, may hold values from -1.5 to 1.5
- mix_bias: float32 [4, 16], replicated, may hold values from -3 to 3
- space_taps: float32 [4, 16, 9], replicated, may hold values from -2.5 to 2.5
- out_weight: bfloat16 [16], replicated, may hold values from -1.5 to 1.5
- out_bias: float32 [1], replicated, may hold values from -3 to 3
Outputs:
- filled: float32 [32, 64, 1024], P(None, 'day', 'tile')
Inputs may be any that keep to these rules, and one draw needn't show every extreme that they name: `granule_list`: on each day and band the 8 owners of a day group name every tile once; one owner names one tile for one band on at most 1 days; offset + count <= 16; on each band some tile has count 16 on every day.
All inputs are finite; a program needn't handle non-finite values. No bound on the sum of `land_mask` on one device may be relied on, other than what follows from the above.
Results may differ from a plain program's by a relative error of at most 0.011.
Values may be sent and summed in bfloat16 or wider, within the bound.
No kernel may reach another device: no remote copies, remote signals or barrier semaphores. Data moves between devices by JAX's collectives and lax.ppermute only.
A program may use at most 64 MiB of HBM per device.

v0:
```python
import functools

import jax
import jax.numpy as jnp
from jax import lax
from jax.experimental import pallas as pl
from jax.experimental.pallas import tpu as pltpu
from jax.sharding import PartitionSpec as P

BF = jnp.bfloat16
F32 = jnp.float32
HALO = 4
LANES = 128
VMEM = pl.BlockSpec(memory_space=pltpu.VMEM)
SMEM = pl.BlockSpec(memory_space=pltpu.SMEM)
ANY = pl.BlockSpec(memory_space=pl.ANY)


def iota(shape, dim):
    return lax.broadcasted_iota(jnp.int32, shape, dim)


def pack_kernel(tiles, bands, days, scene_ref, list_ref, out_ref, wide, mixed, blocks, picked, tail):
    variables, slots = scene_ref.shape[0], scene_ref.shape[1]

    def clear(i, c):
        out_ref[i] = jnp.zeros(out_ref.shape[1:], BF)
        return c

    lax.fori_loop(0, out_ref.shape[0], clear, 0)

    def clear_tail(i, c):
        tail[i] = jnp.zeros((8, LANES), F32)
        return c

    lax.fori_loop(0, tail.shape[0], clear_tail, 0)
    for v in range(variables):
        wide[v, 0:16] = jnp.zeros((16, LANES), F32)
        wide[v, 16 : 16 + slots] = scene_ref[v].astype(F32)
        wide[v, 16 + slots : 32 + slots] = jnp.zeros((16, LANES), F32)
    row = iota((16, LANES), 0)

    def place(day, first):
        for band in range(bands):
            base = (day * bands + band) * 3
            tile, offset, count = list_ref[base], list_ref[base + 1], list_ref[base + 2]
            live = (row >= offset) & (row < offset + count)
            for v in range(variables):
                rows = wide[v, pl.ds(16 + first - offset, 16), :]
                mixed[band, pl.ds(v, 16, stride=4), :] = jnp.where(live, rows, 0.0)
            block = mixed[band].astype(BF)
            blocks[day * bands + band] = block
            out_ref[band * tiles + tile, 16:80] = block
            if band + 1 < bands:
                out_ref[(band + 1) * tiles + tile, 0:16] = block[48:64]
            if band > 0:
                out_ref[(band - 1) * tiles + tile, 80:96] = block[0:16]
            first = first + count
        return first

    lax.fori_loop(0, days, place, jnp.int32(0))

    q, lane = iota((LANES, LANES), 0), iota((LANES, LANES), 1)
    edge = lane % 8
    choose = (q == jnp.where(edge < 4, 124 + edge, edge - 4)).astype(F32).astype(BF)
    granules = days * bands
    spread = jnp.dot(
        blocks[...].reshape(granules * 64, LANES), choose, preferred_element_type=F32
    ).reshape(granules, 64, LANES)
    r64, l64 = iota((64, LANES), 0), iota((64, LANES), 1)
    own = (r64 % 4 == l64 // 32) & ((r64 // 4) % 4 == (l64 % 32) // 8)
    for g in range(granules):
        kept = jnp.where(own, spread[g], 0.0)
        part = [jnp.sum(kept[16 * j : 16 * j + 16], axis=0, keepdims=True) for j in range(4)]
        zero = jnp.zeros((2, LANES), F32)
        picked[g] = jnp.concatenate([part[3], part[0], part[1], part[2], part[3], part[0], zero], 0)

    sub, col = iota((8, LANES), 0), iota((8, LANES), 1)
    row_of = {0: (sub >= 1) & (sub <= 4), 1: sub == 0, -1: sub == 5}
    is_left = col % 8 < 4
    day_base = list_ref[days * bands * 3] * days

    def tags(day, c):
        for band in range(bands):
            base = (day * bands + band) * 3
            tile, offset, count = list_ref[base], list_ref[base + 1], list_ref[base + 2]
            sides = picked[day * bands + band]
            for step, shift, low, high, region in ((0, 4, 0, 16, 1), (1, -12, 12, 16, 0), (-1, 20, 0, 4, 2)):
                lo, hi = jnp.maximum(offset, low), jnp.minimum(offset + count, high)
                for side in range(3):
                    r = col - (24 * side + shift)
                    tag = jnp.where(col == 72 + 3 * side + region, (day_base + day + 1).astype(F32), 0.0)
                    note = jnp.where(sub == 6, jnp.where((r >= lo) & (r < hi), 1.0, tag), 0.0)
                    if side > 0:
                        wanted = row_of[step] & (is_left if side == 1 else jnp.logical_not(is_left))
                        note = note + jnp.where(wanted, sides, 0.0)
                    at = (band + step + 1) * (tiles + 2) + tile + (1, 2, 0)[side]
                    tail[at] = tail[at] + note
        return c

    lax.fori_loop(0, days, tags, 0)
    for band in range(bands):

        def finish(tile, c, band=band):
            out_ref[band * tiles + tile, 96:104] = tail[(band + 1) * (tiles + 2) + tile + 1].astype(BF)
            return c

        lax.fori_loop(0, tiles, finish, 0)


def banded_kernel(width, taps_ref, out_ref):
    at = pl.program_id(0)
    taps = [taps_ref[at * 9 + k] for k in range(9)]
    delta = [(k // 3 - 1) * width + k % 3 - 1 for k in range(9)]
    offset = iota((16, LANES), 0) - iota((16, LANES), 1)
    for k0 in range(0, 768, 16):
        for n0 in range(0, 256, LANES):
            value = jnp.zeros((16, LANES), F32)
            for tap, d in zip(taps, delta):
                want = d + 256 - k0 + n0
                if -(LANES - 1) <= want <= 15:
                    value = jnp.where(offset == want, tap, value)
            out_ref[0, k0 : k0 + 16, n0 : n0 + LANES] = value.astype(BF)


def chunked(low, high, step, fn):
    count = (high - low) // step
    spare = (high - low) - count * step
    for i in range(low, low + spare):
        fn(i)

    def body(i, c):
        for u in range(step):
            fn(low + spare + i * step + u)
        return c

    lax.fori_loop(0, count, body, 0)


def main_kernel(
    sources,
    arrived_ref,
    land_ref,
    valid_ref,
    own_land_ref,
    expand_ref,
    in_ref,
    first_ref,
    rest_ref,
    bias_ref,
    out_w_ref,
    out_b_ref,
    banded_ref,
    out_ref,
    x_ref,
    v_ref,
    taps,
    y_ref,
    sem,
):
    channels = banded_ref.shape[1]
    layers = banded_ref.shape[0]
    width = LANES + 2 * HALO
    rows_in = 24

    def fetch(l):
        return pltpu.make_async_copy(banded_ref.at[l], taps.at[l % 2], sem.at[l % 2])

    fetch(0).start()
    fetch(1).start()

    tail = arrived_ref[:, 96:104, :].astype(F32).reshape(8 * sources, LANES).astype(BF)
    pick_r, pick_c = iota((7 * sources, 8 * sources), 0), iota((7 * sources, 8 * sources), 1)
    pick = ((pick_c // 8 == pick_r % sources) & (pick_c % 8 == pick_r // sources)).astype(F32).astype(BF)
    parts = jnp.dot(pick, tail, preferred_element_type=F32).astype(BF)
    side_rows = [parts[j * sources : (j + 1) * sources] for j in range(6)]
    meta = parts[6 * sources :]
    wanted = (iota((16, LANES), 1) == iota((16, LANES), 0) + 72).astype(F32).astype(BF)
    tag_rows = lax.dot_general(wanted, meta, (((1,), (1,)), ((), ())), preferred_element_type=F32)
    repeat = (iota((sources, 8 * sources), 1) // 8 == iota((sources, 8 * sources), 0)).astype(F32).astype(BF)
    tag_wide = jnp.dot(tag_rows.astype(BF), repeat, preferred_element_type=F32)
    m, k = iota((256, 8 * sources), 0), iota((256, 8 * sources), 1)
    same = m // 32 == k % 8
    day_of = (m % 32 + 1).astype(F32)
    perms = [
        jnp.where(same & (tag_wide[b : b + 1] == day_of), 1.0, 0.0).astype(BF) for b in range(3)
    ]
    day_col = (iota((32, sources), 0) + 1).astype(F32)
    hot = [jnp.where(tag_rows[i : i + 1] == day_col, 1.0, 0.0).astype(BF) for i in range(9)]

    lane32 = iota((32, LANES), 1)
    cover = jnp.zeros((32, LANES), F32)
    for side in range(3):
        for band, (lo, hi) in enumerate(((0, 4), (4, 20), (20, 24))):
            got = jnp.dot(hot[3 * side + band], meta, preferred_element_type=F32)
            here = (lane32 >= 24 * side + lo) & (lane32 < 24 * side + hi)
            cover = jnp.where(here, got, cover)
    cover = cover.astype(BF)

    packed = [[None] * 2 for _ in range(4)]
    for j in range(6):
        band = 0 if j == 0 else (2 if j == 5 else 1)
        left = jnp.dot(hot[3 + band], side_rows[j], preferred_element_type=F32)
        right = jnp.dot(hot[6 + band], side_rows[j], preferred_element_type=F32)
        both = jnp.where(lane32 % 8 < 4, left, right)
        half, start = (32 * j) // LANES, (32 * j) % LANES
        here = (lane32 >= start) & (lane32 < start + 32)
        for v in range(4):
            moved = pltpu.roll(both, (start - 32 * v) % LANES, 1)
            had = packed[v][half]
            packed[v][half] = jnp.where(here, moved, 0.0 if had is None else had)
    edges = [jnp.concatenate([packed[v][h] for v in range(4)], 0) for h in range(2)]

    rolled = []
    for p in range(12):
        band = 0 if p < 2 else (2 if p >= 10 else 1)
        rows = arrived_ref[:, 8 * p : 8 * p + 8, :].astype(F32).reshape(8 * sources, LANES).astype(BF)
        got = jnp.dot(perms[band], rows, preferred_element_type=F32)
        for r2 in range(2):
            row = 2 * p + r2
            rolled.append(pltpu.roll(got[128 * r2 : 128 * r2 + 128], (8 * row + 4) % LANES, 1))
    lane = iota((LANES, LANES), 1)
    zero = jnp.zeros((LANES, LANES), F32)

    def flat_block(b):
        now, start = (b, 8 * b + 4) if b <= 15 else ((b - 1, 8 * b - 132) if b >= 17 else (16, 132))
        before = now - 1
        now_v = rolled[now] if now < rows_in else zero
        before_v = rolled[before] if before >= 0 else zero
        edge = edges[0] if b <= 16 else edges[1]
        return jnp.where(lane < start - 8, before_v, jnp.where(lane < start, edge, now_v))

    for j in range(13):
        pair = []
        for b in (2 * j, 2 * j + 1):
            keep = jnp.dot(cover, expand_ref[b], preferred_element_type=F32)
            pair.append((jnp.concatenate([flat_block(b), keep, keep], 0) * land_ref[b : b + 1]).astype(BF))
        got = jnp.dot(in_ref[...], jnp.concatenate(pair, 1), preferred_element_type=F32).astype(BF)
        x_ref[2 * j] = got[:, :LANES]
        x_ref[2 * j + 1] = got[:, LANES:]

    for b in (0, 1, 28, 29):
        v_ref[b] = jnp.zeros(v_ref.shape[1:], BF)

    def mix(l, j):
        both = jnp.concatenate([x_ref[2 * j], x_ref[2 * j + 1]], 1)
        ok = jnp.concatenate([valid_ref[pl.ds(2 * j, 1)], valid_ref[pl.ds(2 * j + 1, 1)]], 1)
        bias = bias_ref[l]
        for p in range(2):
            half = slice(256 * p, 256 * p + 256)
            if l == 0:
                acc = jnp.dot(first_ref[half], both, preferred_element_type=F32)
            else:
                acc = jnp.dot(rest_ref[l - 1, p], both[half], preferred_element_type=F32)
            h = acc + jnp.concatenate([bias[half], bias[half]], 1)
            v = ((h + h * jnp.tanh(h)) * ok).astype(BF)
            v_ref[2 * j + 2, half] = v[:, :LANES]
            v_ref[2 * j + 3, half] = v[:, LANES:]

    def stencil(l, low, high, c):
        groups = [pl.ds(pl.multiple_of(c * 16 + 256 * p, 16), 16) for p in range(2)]
        lhs = jnp.concatenate(
            [
                jnp.concatenate([v_ref[2 * j + b, rows] for b in range(6)], 1)
                for j in range(low, high)
                for rows in groups
            ],
            0,
        )
        acc = jnp.dot(lhs, taps[l % 2, c], preferred_element_type=F32)
        at = 0
        for j in range(low, high):
            for rows in groups:
                for h in range(2):
                    part = acc[at : at + 16, LANES * h : LANES * h + LANES]
                    x_ref[2 * j + h, rows] = (x_ref[2 * j + h, rows].astype(F32) + part).astype(BF)
                at += 16

    for l in range(layers):
        low_v, high_v = l * width // 256, -(-(rows_in - l) * width // 256)
        low_x, high_x = (l + 1) * width // 256, -(-(rows_in - l - 1) * width // 256)
        chunked(low_v, high_v, 4, functools.partial(mix, l))
        fetch(l).wait()
        chunked(0, channels, 4, functools.partial(stencil, l, low_x, high_x))
        if l + 2 < layers:
            fetch(l + 2).start()

    for j in range(2, 11):
        got = jnp.dot(
            out_w_ref[...], jnp.concatenate([x_ref[2 * j], x_ref[2 * j + 1]], 1), preferred_element_type=F32
        )
        y_ref[2 * j] = got[:, :LANES]
        y_ref[2 * j + 1] = got[:, LANES:]
    lane_d = iota((32, LANES), 1)
    for r in range(16):
        block, start = divmod((r + HALO) * width + HALO, LANES)
        back = (LANES - start) % LANES
        value = pltpu.roll(y_ref[block], back, 1) if back else y_ref[block]
        if start:
            value = jnp.where(lane_d < LANES - start, value, pltpu.roll(y_ref[block + 1], back, 1))
        out_ref[:, r, :] = (value + out_b_ref[0]) * own_land_ref[r : r + 1]


def local(
    scene_rows,
    granule_list,
    land_mask,
    in_weight,
    obs_bias,
    time_taps,
    mix_weight,
    mix_bias,
    space_taps,
    out_weight,
    out_bias,
):
    bands = lax.axis_size("day")
    tiles = lax.axis_size("tile")
    days_here = granule_list.shape[0]
    days = days_here * bands
    rows, cols = land_mask.shape
    channels, variables = in_weight.shape
    layers = mix_weight.shape[0]
    sources = bands * tiles
    width = cols + 2 * HALO
    tall = rows + 2 * HALO
    band_at, tile_at = lax.axis_index("day"), lax.axis_index("tile")
    slots = scene_rows.shape[3]
    n_block = 26

    notes = jnp.concatenate([granule_list.reshape(-1), band_at.reshape(1).astype(jnp.int32)])
    granules = days_here * bands
    outgoing = pl.pallas_call(
        functools.partial(pack_kernel, tiles, bands, days_here),
        out_shape=jax.ShapeDtypeStruct((sources, 104, cols), BF),
        in_specs=[VMEM, SMEM],
        out_specs=VMEM,
        scratch_shapes=[
            pltpu.VMEM((variables, slots + 32, cols), F32),
            pltpu.VMEM((bands, 64, cols), F32),
            pltpu.VMEM((granules, 64, cols), BF),
            pltpu.VMEM((granules, 8, cols), F32),
            pltpu.VMEM(((bands + 2) * (tiles + 2), 8, cols), F32),
        ],
        compiler_params=pltpu.CompilerParams(vmem_limit_bytes=32 * 2**20),
        name="pack",
    )(scene_rows.reshape(variables, slots, cols), notes)
    arrived = lax.all_to_all(outgoing, ("day", "tile"), split_axis=0, concat_axis=0, tiled=True)

    half = days // 2
    order = jnp.arange(2 * channels * half)
    ch_of = (order // half) % channels
    day_of = 2 * (order % half) + order // (channels * half)
    gap = day_of[None, :] - day_of[:, None]
    pair = [mix_weight[l].astype(F32)[ch_of][:, ch_of] for l in range(0)]
    del pair

    def day_matrix(l, n_par):
        spacing = 2**l
        w = 0.5 * mix_weight[l].astype(F32)[:, :, None] * time_taps[l][None, :, :]
        d = 2 * jnp.arange(half)[None, :] + jnp.arange(2)[:, None]
        diff = d[None, None, :, :] - d[:, :, None, None]
        hit = jnp.stack([(diff == (k - 1) * spacing).astype(F32) for k in range(3)], -1)
        full = sum(
            w[None, :, None, None, :, None, k] * hit[:, None, :, :, None, :, k] for k in range(3)
        )
        return full.astype(BF)

    first = day_matrix(0, 2).reshape(channels * days, channels * days)
    rest = jnp.stack(
        [
            jnp.stack(
                [
                    day_matrix(l, 2)[p, :, :, p].reshape(channels * half, channels * half)
                    for p in range(2)
                ]
            )
            for l in range(1, layers)
        ]
    )
    by_row = lambda a: jnp.broadcast_to(a[..., None, :, None], a.shape[:-1] + (2, channels, half)).reshape(
        a.shape[:-1] + (channels * days,)
    )
    bias = jnp.broadcast_to(0.5 * by_row(mix_bias)[..., None], (layers, channels * days, LANES))
    same_day = (day_of[:, None] == jnp.arange(days)[None, :]).astype(F32)
    bias_hi = obs_bias.astype(BF).astype(F32)
    in_cols = [by_row(in_weight[:, v].astype(F32))[:, None] * same_day for v in range(variables)]
    in_cols += [by_row(b)[:, None] * same_day for b in (bias_hi, obs_bias - bias_hi)]
    in_full = jnp.concatenate(in_cols, 1).astype(BF)
    out_full = (by_row(out_weight.astype(F32))[:, None] * same_day).T.astype(BF)

    banded = pl.pallas_call(
        functools.partial(banded_kernel, width),
        grid=(layers * channels,),
        out_shape=jax.ShapeDtypeStruct((layers * channels, 768, 256), BF),
        in_specs=[SMEM],
        out_specs=pl.BlockSpec((1, 768, 256), lambda i: (i, 0, 0)),
        cost_estimate=pl.CostEstimate(
            flops=64 * 768 * 256 * 8, bytes_accessed=64 * 768 * 256 * 2, transcendentals=0
        ),
        name="banded",
    )(space_taps.reshape(-1)).reshape(layers, channels, 768, 256)

    forward = lambda n: [(i, i + 1) for i in range(n - 1)]
    backward = lambda n: [(i + 1, i) for i in range(n - 1)]
    land = land_mask.astype(BF)
    land = jnp.concatenate(
        [
            lax.ppermute(land[rows - HALO :], "day", forward(bands)),
            land,
            lax.ppermute(land[:HALO], "day", backward(bands)),
        ],
        0,
    )
    land = jnp.concatenate(
        [
            lax.ppermute(land[:, cols - HALO :], "tile", forward(tiles)),
            land,
            lax.ppermute(land[:, :HALO], "tile", backward(tiles)),
        ],
        1,
    ).astype(F32)
    r, q = jnp.arange(tall)[:, None], jnp.arange(width)[None, :]
    outside = ((r < HALO) & (band_at == 0)) | ((r >= rows + HALO) & (band_at == bands - 1))
    outside = outside | ((q < HALO) & (tile_at == 0)) | ((q >= cols + HALO) & (tile_at == tiles - 1))
    valid = jnp.where(outside, 0.0, 1.0)
    flat = lambda a: jnp.pad(a.reshape(-1), (0, n_block * LANES - tall * width)).reshape(n_block, LANES)
    position = jnp.arange(n_block * LANES).reshape(n_block, 1, LANES)
    region = jnp.where(position % width < HALO, 1, jnp.where(position % width >= cols + HALO, 2, 0))
    slot = jnp.where(position < tall * width, 24 * region + position // width, -1)
    expand = (slot == jnp.arange(LANES)[None, :, None]).astype(BF)

    return pl.pallas_call(
        functools.partial(main_kernel, sources),
        out_shape=jax.ShapeDtypeStruct((days, rows, cols), F32),
        in_specs=[VMEM] * 10 + [SMEM, ANY],
        out_specs=VMEM,
        scratch_shapes=[
            pltpu.VMEM((n_block, channels * days, LANES), BF),
            pltpu.VMEM((n_block + 4, channels * days, LANES), BF),
            pltpu.VMEM((2, channels, 768, 256), BF),
            pltpu.VMEM((n_block, days, LANES), F32),
            pltpu.SemaphoreType.DMA((2,)),
        ],
        compiler_params=pltpu.CompilerParams(vmem_limit_bytes=44 * 2**20),
        name="blocks",
    )(
        arrived,
        flat(land),
        flat(valid),
        land_mask.astype(F32),
        expand,
        in_full,
        first,
        rest,
        bias,
        out_full,
        out_bias,
        banded,
    )


def solution(mesh):
    placed = (
        P(None, "day", "tile", None, None),
        P("day", "tile", None, None),
        P("day", "tile"),
        P(),
        P(),
        P(),
        P(),
        P(),
        P(),
        P(),
        P(),
    )
    return jax.shard_map(
        local, mesh=mesh, in_specs=placed, out_specs=P(None, "day", "tile"), check_vma=False
    )
```

profile of v0, /device:TPU:19, one launch (start us, length us, event | category | flops | bytes accessed | tf_op | source)
XLA Modules:
  0.0 142.1 jit_solution(18347888345033127685)
XLA Ops:
  0.0 0.8 fusion.34
  1.4 3.1 %collective-permute-start = (bf16[4,128]{1,0:T(4,128)(2,1)}, bf16[4,128]{1,0:T(4,128)(2,1)}, u32[]{:S(2)}, u32[]{:S(2)}) collective-permute-start(bf16[4,128]{1,0:T(4,128)(2,1)} %get-tuple-element.38), channel_id=1, source_target_pairs={{0,8},{8,16},{16,24},{1,9},{9,17},{17,25},{2,10},{10,18},{18,26},{... | collective-permute-start | bytes 3080 | tf_op jit(solution)/shard_map/ppermute | solution.py:409
  4.5 2.7 %collective-permute-start.1 = (bf16[4,128]{1,0:T(4,128)(2,1)}, bf16[4,128]{1,0:T(4,128)(2,1)}, u32[]{:S(2)}, u32[]{:S(2)}) collective-permute-start(bf16[4,128]{1,0:T(4,128)(2,1)} %get-tuple-element.39), channel_id=1, source_target_pairs={{8,0},{16,8},{24,16},{9,1},{17,9},{25,17},{10,2},{18,10},{26,18},{... | collective-permute-start | bytes 3080 | tf_op jit(solution)/shard_map/ppermute | solution.py:411
  7.2 0.8 copy.14
  8.2 1.0 copy-done
  9.3 3.3 %pack.1 = bf16[32,104,128]{2,1,0:T(8,128)(2,1)} custom-call(bf16[4,512,128]{2,1,0:T(8,128)(2,1)S(1)} %bitcast.96, s32[97]{0:T(128)S(1)} %pad_add_fusion.list_ref), custom_call_target="tpu_custom_call" | custom-call | tf_op jit(solution)/shard_map/pack/pallas_call | solution.py:333
  12.5 6.7 %all-to-all-start = ((bf16[32,104,128]{2,1,0:T(8,128)(2,1)}), bf16[32,104,128]{2,1,0:T(8,128)(2,1)S(1)}, u32[]{:S(2)}, u32[]{:S(2)}) async-start(bf16[32,104,128]{2,1,0:T(8,128)(2,1)} %pack.1), calls=%async_computation | async-start | bytes 1703936 | tf_op jit(solution)/shard_map/all_to_all | solution.py:348
  19.9 1.2 fusion.30
  21.1 1.3 broadcast_multiply_fusion.4
  22.4 1.4 %bitcast_convert_fusion.1 = (bf16[16]{0:T(256)(128)(2,1)}, bf16[16]{0:T(256)(128)(2,1)}, bf16[16]{0:T(256)(128)(2,1)}, bf16[16]{0:T(256)(128)(2,1)}) fusion(bf16[16,4]{0,1:T(4,128)(2,1)} %param.14), kind=kLoop, calls=%fused_computation.101 | loop fusion | bytes 256 | tf_op jit(solution)/shard_map/convert_element_type | solution.py:387
  23.8 0.8 fusion.35
  24.7 0.7 broadcast_in_dim.44
  25.4 0.7 mul.626
  26.2 0.7 select_n.103
  26.9 0.7 multiply_bitcast_fusion.2
  28.3 0.7 fusion.4
  29.0 7.6 %add_convert_fusion.2 = (bf16[2,16,16,2,16,16]{5,4,2,1,3,0:T(8,128)(2,1)S(1)}, bf16[2,16,16,2,16,16]{5,4,2,1,3,0:T(8,128)(2,1)}, bf16[2,16,16,2,16,16]{5,4,2,1,3,0:T(8,128)(2,1)}) fusion(f32[2,16,2,16]{3,1,2,0:T(8,128)S(1)} %get-tuple-element.50, f32[16,16]{1,0:T(8,128)S(1)} %get-tuple-element.15, f32[16,16]{1,0:T(8,128)S(1)} %get-tuple-element.16, ...), kind=kLoop, calls=%fused_computation.2 | loop fusion | flops 4718592 | bytes 1610752 | tf_op jit(solution)/shard_map/convert_element_type | solution.py:367
  37.1 1.0 stack_reshape_squeeze.18
  38.1 1.0 stack_reshape_squeeze.19
  39.1 1.9 %fusion.32 = (bf16[1,16,16,1,16,16]{5,4,2,1,3,0:T(8,128)(2,1)S(1)}, bf16[1,16,16,1,16,16]{5,4,2,1,3,0:T(8,128)(2,1)S(1)}) fusion(bf16[2,16,16,2,16,16]{5,4,2,1,3,0:T(8,128)(2,1)} %get-tuple-element.12), kind=kLoop, calls=%fused_computation.109 | loop fusion | bytes 524288 | tf_op jit(solution)/shard_map/slice | solution.py:374
  41.0 1.0 stack_reshape_squeeze.20
  42.0 1.0 stack_reshape_squeeze.21
  43.0 1.9 %fusion.33 = (bf16[1,16,16,1,16,16]{5,4,2,1,3,0:T(8,128)(2,1)S(1)}, bf16[1,16,16,1,16,16]{5,4,2,1,3,0:T(8,128)(2,1)S(1)}) fusion(bf16[2,16,16,2,16,16]{5,4,2,1,3,0:T(8,128)(2,1)} %get-tuple-element.13), kind=kLoop, calls=%fused_computation.110 | loop fusion | bytes 524288 | tf_op jit(solution)/shard_map/slice | solution.py:374
  44.9 1.7 %stack_reshape_squeeze.22 = bf16[1,256,256]{2,1,0:T(8,128)(2,1)} reshape(bf16[1,16,16,1,16,16]{5,4,2,1,3,0:T(8,128)(2,1)S(1)} %get-tuple-element.9) | data formatting | bytes 262144 | tf_op jit(solution)/shard_map/stack;reshape;squeeze | solution.py:372
  46.6 1.0 stack_reshape_squeeze.23
  47.6 0.7 select_convert_fusion.6.out_w_ref
  48.3 0.9 maximum_bitcast_fusion.2
  49.3 0.7 pad_bitcast_fusion.valid_ref
  50.0 0.7 convert_element_type.270
  50.7 0.7 broadcast_in_dim.39
  52.3 0.7 broadcast_in_dim.37
  53.1 0.8 broadcast_in_dim.36
  54.0 0.7 broadcast_in_dim.38
  54.8 0.8 copy.16
  55.6 0.7 reshape.332.taps_ref
  56.4 1.3 select_convert_fusion
  57.8 0.9 fusion.expand_ref
  58.7 4.6 %add_convert_fusion.3 = bf16[2,16,16,2,16,16]{5,4,2,1,3,0:T(8,128)(2,1)} fusion(f32[2,16,2,16]{3,1,2,0:T(8,128)S(1)} %get-tuple-element.51, f32[16,16]{1,0:T(8,128)} %get-tuple-element.24, f32[2,16,2,16]{3,1,2,0:T(8,128)S(1)} %get-tuple-element.52, f32[16,16]{1,0:T(8,128)} %get-tuple-element.25, f32[2,16,2,16]{3,1,2,0:T(8,128)} %get-tuple-element.53, ...), kind=kLoop, calls=%fused_computation.3 | loop fusion | flops 1572864 | bytes 539648 | tf_op jit(solution)/shard_map/convert_element_type | solution.py:367
  63.3 27.5 %banded.1 = bf16[64,768,256]{2,1,0:T(8,128)(2,1)} custom-call(f32[576]{0:T(1024)} %reshape.332.taps_ref), custom_call_target="tpu_custom_call" | custom-call | flops 100663296 | bytes 25165824 | tf_op jit(solution)/shard_map/banded/pallas_call | solution.py:392
  91.6 5.0 %copy.15 = bf16[2,16,16,2,16,16]{5,4,3,2,1,0:T(8,128)(2,1)} copy(bf16[2,16,16,2,16,16]{5,4,2,1,3,0:T(8,128)(2,1)} %add_convert_fusion.3) | data formatting | bytes 1048576 | tf_op jit(solution)/shard_map/convert_element_type | solution.py:367
  96.6 7.8 %convert_element_type.226.first_ref = bf16[512,512]{1,0:T(8,128)(2,1)S(1)} reshape(bf16[2,16,16,2,16,16]{5,4,3,2,1,0:T(8,128)(2,1)} %copy.15) | data formatting | bytes 1048576 | tf_op jit(solution)/shard_map/convert_element_type | solution.py:367
  104.4 0.7 pad_maximum_fusion.2
  105.2 3.4 %collective-permute-start.2 = (bf16[24,4]{1,0:T(8,128)(2,1)S(1)}, bf16[24,4]{1,0:T(8,128)(2,1)S(1)}, u32[]{:S(2)}, u32[]{:S(2)}) collective-permute-start(bf16[24,4]{1,0:T(8,128)(2,1)S(1)} %get-tuple-element.36), channel_id=1, source_target_pairs={{0,1},{1,2},{2,3},{3,4},{4,5},{5,6},{6,7},{8,9},{9,10},{10,11},{11... | collective-permute-start | bytes 584 | tf_op jit(solution)/shard_map/ppermute | solution.py:417
  108.6 1.9 %collective-permute-start.3 = (bf16[24,4]{1,0:T(8,128)(2,1)S(1)}, bf16[24,4]{1,0:T(8,128)(2,1)S(1)}, u32[]{:S(2)}, u32[]{:S(2)}) collective-permute-start(bf16[24,4]{1,0:T(8,128)(2,1)S(1)} %get-tuple-element.37), channel_id=1, source_target_pairs={{1,0},{2,1},{3,2},{4,3},{5,4},{6,5},{7,6},{9,8},{10,9},{11,10},{12... | collective-permute-start | bytes 584 | tf_op jit(solution)/shard_map/ppermute | solution.py:419
  110.5 1.4 concatenate.16.in_ref
  111.9 1.6 %collective-permute-done.3 = bf16[24,4]{1,0:T(8,128)(2,1)S(1)} collective-permute-done((bf16[24,4]{1,0:T(8,128)(2,1)S(1)}, bf16[24,4]{1,0:T(8,128)(2,1)S(1)}, u32[]{:S(2)}, u32[]{:S(2)}) %collective-permute-start.3) | collective-permute-done | bytes 224 | tf_op jit(solution)/shard_map/ppermute | solution.py:419
  113.5 0.8 pad_maximum_fusion.1
  114.8 27.1 %blocks.1 = f32[32,16,128]{2,1,0:T(8,128)} custom-call(bf16[32,104,128]{2,1,0:T(8,128)(2,1)S(1)} %all-to-all-done.arrived_ref, f32[26,128]{1,0:T(8,128)S(1)} %bitcast_convert_fusion.land_ref, f32[26,128]{1,0:T(8,128)S(1)} %pad_bitcast_fusion.valid_ref, f32[16,128]{1,0:T(8,128)S(1)} %get-tuple-element.30.own_land_ref, ...), custom_call_target="tpu_custom_call" | custom-call | tf_op jit(solution)/shard_map/blocks/pallas_call | solution.py:433
  (45 shorter events, 4.8 us)
Async XLA Ops:
  1.4 103.0 %collective-permute-start = (bf16[4,128]{1,0:T(4,128)(2,1)}, bf16[4,128]{1,0:T(4,128)(2,1)}, u32[]{:S(2)}, u32[]{:S(2)}) collective-permute-start(bf16[4,128]{1,0:T(4,128)(2,1)} %get-tuple-element.38), channel_id=1, source_target_pairs={{0,8},{8,16},{16,24},{1,9},{9,17},{17,25},{2,10},{10,18},{18,26},{... | collective-permute-start | bytes 3080 | tf_op jit(solution)/shard_map/ppermute | solution.py:409
  4.5 99.9 %collective-permute-start.1 = (bf16[4,128]{1,0:T(4,128)(2,1)}, bf16[4,128]{1,0:T(4,128)(2,1)}, u32[]{:S(2)}, u32[]{:S(2)}) collective-permute-start(bf16[4,128]{1,0:T(4,128)(2,1)} %get-tuple-element.39), channel_id=1, source_target_pairs={{8,0},{16,8},{24,16},{9,1},{17,9},{25,17},{10,2},{18,10},{26,18},{... | collective-permute-start | bytes 3080 | tf_op jit(solution)/shard_map/ppermute | solution.py:411
  8.2 1.0 copy-start
  12.5 101.9 %all-to-all-start = ((bf16[32,104,128]{2,1,0:T(8,128)(2,1)}), bf16[32,104,128]{2,1,0:T(8,128)(2,1)S(1)}, u32[]{:S(2)}, u32[]{:S(2)}) async-start(bf16[32,104,128]{2,1,0:T(8,128)(2,1)} %pack.1), calls=%async_computation | async-start | bytes 1703936 | tf_op jit(solution)/shard_map/all_to_all | solution.py:348
  63.2 28.2 %copy-start.1 = (f32[4,16]{1,0:T(4,128)S(1)}, f32[4,16]{1,0:T(4,128)}, u32[]{:S(2)}) copy-start(f32[4,16]{1,0:T(4,128)} %broadcast_multiply_fusion.4) | copy-start | bytes 772
  105.2 6.8 %collective-permute-start.2 = (bf16[24,4]{1,0:T(8,128)(2,1)S(1)}, bf16[24,4]{1,0:T(8,128)(2,1)S(1)}, u32[]{:S(2)}, u32[]{:S(2)}) collective-permute-start(bf16[24,4]{1,0:T(8,128)(2,1)S(1)} %get-tuple-element.36), channel_id=1, source_target_pairs={{0,1},{1,2},{2,3},{3,4},{4,5},{5,6},{6,7},{8,9},{9,10},{10,11},{11... | collective-permute-start | bytes 584 | tf_op jit(solution)/shard_map/ppermute | solution.py:417
  108.6 4.9 %collective-permute-start.3 = (bf16[24,4]{1,0:T(8,128)(2,1)S(1)}, bf16[24,4]{1,0:T(8,128)(2,1)S(1)}, u32[]{:S(2)}, u32[]{:S(2)}) collective-permute-start(bf16[24,4]{1,0:T(8,128)(2,1)S(1)} %get-tuple-element.37), channel_id=1, source_target_pairs={{1,0},{2,1},{3,2},{4,3},{5,4},{6,5},{7,6},{9,8},{10,9},{11,10},{12... | collective-permute-start | bytes 584 | tf_op jit(solution)/shard_map/ppermute | solution.py:419
where the time goes:
time: 144 us; the launch traced here: 142 us
  Pallas kernels  57.9 us (40%)
  local copies, waits for them, and re-layouts  39.7 us (28%)
  other arithmetic  23.9 us (17%)
  starting transfers between devices  17.9 us (12%)
  waiting for transfers between devices  1.6 us (1%)
    pallas_call x1, Pallas kernels, local(): pl.pallas_call(functools.partial(banded_kernel, width), grid=(layers * ch...  27.5 us
    pallas_call x1, Pallas kernels, local(): pl.pallas_call(functools.partial(main_kernel, sources), out_shape=jax.Sha...  27.1 us
    convert_element_type x2, local copies, waits for them, and re-layouts, day_matrix(): return full.astype(BF)  12.8 us
    convert_element_type x2, other arithmetic, day_matrix(): return full.astype(BF)  12.2 us
    all_to_all x1, starting transfers between devices, local(): lax.all_to_all(outgoing, ('day', 'tile'), split_axis=0, concat_axis=0, ti...  6.74 us
    another operation x6, local copies, waits for them, and re-layouts, local(): jnp.stack([day_matrix(l, 2)[p, :, :, p].reshape(channels * half, channels...  6.6 us
    broadcast_in_dim x8, local copies, waits for them, and re-layouts, local(): jnp.broadcast_to(a[..., None, :, None], a.shape[:-1] + (2, channels, half))  4.38 us
    slice x3, local copies, waits for them, and re-layouts, local(): day_matrix(l, 2)[p, :, :, p].reshape(channels * half, channels * half)  4.29 us
  transfers between devices with their start and end apart: 5, of which 1 were waited for; matrix products, arithmetic and copies ran while one was open for 43% of the time, Pallas kernels for 22%

commit v1 on v0

--- a/solution.py
+++ b/solution.py
@@ -13,15 +13,18 @@
 LANES = 128
 VMEM = pl.BlockSpec(memory_space=pltpu.VMEM)
 SMEM = pl.BlockSpec(memory_space=pltpu.SMEM)
-ANY = pl.BlockSpec(memory_space=pl.ANY)
+HBM = pl.BlockSpec(memory_space=pltpu.HBM)
 
 
 def iota(shape, dim):
     return lax.broadcasted_iota(jnp.int32, shape, dim)
 
 
-def pack_kernel(tiles, bands, days, scene_ref, list_ref, out_ref, wide, mixed, blocks, picked, tail):
+def pack_kernel(tiles, bands, days, scene_ref, list_ref, out_ref, scene, wide, mixed, blocks, picked, tail, sem):
     variables, slots = scene_ref.shape[0], scene_ref.shape[1]
+    copies = [pltpu.make_async_copy(scene_ref.at[v], scene.at[v], sem.at[v]) for v in range(variables)]
+    for copy in copies:
+        copy.start()
 
     def clear(i, c):
         out_ref[i] = jnp.zeros(out_ref.shape[1:], BF)
@@ -36,14 +39,14 @@
     lax.fori_loop(0, tail.shape[0], clear_tail, 0)
     for v in range(variables):
         wide[v, 0:16] = jnp.zeros((16, LANES), F32)
-        wide[v, 16 : 16 + slots] = scene_ref[v].astype(F32)
+        copies[v].wait()
+        wide[v, 16 : 16 + slots] = scene[v].astype(F32)
         wide[v, 16 + slots : 32 + slots] = jnp.zeros((16, LANES), F32)
     row = iota((16, LANES), 0)
 
     def place(day, first):
         for band in range(bands):
-            base = (day * bands + band) * 3
-            tile, offset, count = list_ref[base], list_ref[base + 1], list_ref[base + 2]
+            tile, offset, count = (list_ref[k, band, day] for k in range(3))
             live = (row >= offset) & (row < offset + count)
             for v in range(variables):
                 rows = wide[v, pl.ds(16 + first - offset, 16), :]
@@ -78,12 +81,11 @@
     sub, col = iota((8, LANES), 0), iota((8, LANES), 1)
     row_of = {0: (sub >= 1) & (sub <= 4), 1: sub == 0, -1: sub == 5}
     is_left = col % 8 < 4
-    day_base = list_ref[days * bands * 3] * days
+    day_base = lax.axis_index("day") * days
 
     def tags(day, c):
         for band in range(bands):
-            base = (day * bands + band) * 3
-            tile, offset, count = list_ref[base], list_ref[base + 1], list_ref[base + 2]
+            tile, offset, count = (list_ref[k, band, day] for k in range(3))
             sides = picked[day * bands + band]
             for step, shift, low, high, region in ((0, 4, 0, 16, 1), (1, -12, 12, 16, 0), (-1, 20, 0, 4, 2)):
                 lo, hi = jnp.maximum(offset, low), jnp.minimum(offset + count, high)
@@ -108,19 +110,137 @@
         lax.fori_loop(0, tiles, finish, 0)
 
 
-def banded_kernel(width, taps_ref, out_ref):
-    at = pl.program_id(0)
-    taps = [taps_ref[at * 9 + k] for k in range(9)]
+def halves(value):
+    high = value.astype(BF)
+    return high, (value - high.astype(F32)).astype(BF)
+
+
+def place_of(block, width, shape):
+    first = block * LANES // width
+    lane = iota(shape, len(shape) - 1)
+    row = first + (lane >= (first + 1) * width - block * LANES).astype(jnp.int32)
+    return row, lane + block * LANES - row * width
+
+
+def weights_kernel(
+    width,
+    *refs,
+):
+    params, results, held, made, sem = refs[:7], refs[7:15], refs[15:22], refs[22:30], refs[30]
+    copies = [pltpu.make_async_copy(a, b, sem.at[i]) for i, (a, b) in enumerate(zip(params, held))]
+    for copy in copies:
+        copy.start()
+    for copy in copies:
+        copy.wait()
+    weights_body(width, *held, *made)
+    copies = [pltpu.make_async_copy(a, b, sem.at[i]) for i, (a, b) in enumerate(zip(made, results))]
+    for copy in copies:
+        copy.start()
+    for copy in copies:
+        copy.wait()
+
+
+def weights_body(
+    width,
+    taps_ref,
+    time_ref,
+    mix_ref,
+    mix_bias_ref,
+    in_ref,
+    obs_bias_ref,
+    out_ref,
+    band_out,
+    first_out,
+    rest_out,
+    bias_out,
+    in_out,
+    out_out,
+    expand_out,
+    valid_out,
+):
+    layers, channels = mix_ref.shape[0], mix_ref.shape[1]
+    half = first_out.shape[0] // (2 * channels)
+    days = 2 * half
+    size = channels * days
+
     delta = [(k // 3 - 1) * width + k % 3 - 1 for k in range(9)]
     offset = iota((16, LANES), 0) - iota((16, LANES), 1)
-    for k0 in range(0, 768, 16):
-        for n0 in range(0, 256, LANES):
-            value = jnp.zeros((16, LANES), F32)
-            for tap, d in zip(taps, delta):
-                want = d + 256 - k0 + n0
-                if -(LANES - 1) <= want <= 15:
-                    value = jnp.where(offset == want, tap, value)
-            out_ref[0, k0 : k0 + 16, n0 : n0 + LANES] = value.astype(BF)
+
+    def band(at, c):
+        l, ch = at // channels, at % channels
+        taps = [taps_ref[k, l, ch] for k in range(9)]
+        for t in range(5):
+            for k0 in range(0, LANES, 16):
+                value = jnp.zeros((16, LANES), F32)
+                for tap, d in zip(taps, delta):
+                    want = d - LANES * (t - 2) - k0
+                    if -(LANES - 1) <= want <= 15:
+                        value = jnp.where(offset == want, tap, value)
+                band_out[l, ch, t, k0 : k0 + 16] = value.astype(BF)
+        return c
+
+    lax.fori_loop(0, layers * channels, band, 0)
+
+    hot = ((iota((size, channels), 0) // half) % channels == iota((size, channels), 1)).astype(F32).astype(BF)
+    day = lambda n, shape, dim: 2 * (iota(shape, dim) % half) + iota(shape, dim) // (channels * half)
+
+    def widened(l, k, count):
+        mixed = (0.5 * mix_ref[l].astype(F32) * time_ref[k, l : l + 1]).astype(BF)
+        rows = jnp.dot(hot[:count], mixed, preferred_element_type=F32).astype(BF)
+        return lax.dot_general(rows, hot[:count], (((1,), (1,)), ((), ())), preferred_element_type=F32)
+
+    for l in range(layers):
+        count = size if l == 0 else size // 2
+        gap = day(l, (count, count), 1) - day(l, (count, count), 0)
+        value = jnp.zeros((count, count), F32)
+        for k in range(3):
+            value = jnp.where(gap == (k - 1) * 2**l, widened(l, k, count), value)
+        if l == 0:
+            first_out[...] = value.astype(BF)
+        else:
+            rest_out[l - 1] = value.astype(BF)
+
+    rows8 = jnp.concatenate([0.5 * mix_bias_ref[...], obs_bias_ref[...], jnp.zeros((3, channels), F32)], 0)
+    high, rest = halves(rows8)
+    mid, low = halves(rows8 - high.astype(F32))
+    nt = lambda a, b: lax.dot_general(a, b, (((1,), (1,)), ((), ())), preferred_element_type=F32)
+    column = nt(hot, high) + (nt(hot, mid) + nt(hot, low))
+    for l in range(layers):
+        bias_out[l] = jnp.broadcast_to(column[:, l : l + 1], (size, LANES))
+
+    variables = in_ref.shape[0]
+    repeat = (iota((variables, LANES), 1) // days == iota((variables, LANES), 0)).astype(F32).astype(BF)
+    in_row = lax.dot_general(
+        in_ref[...].astype(F32), repeat.astype(F32), (((0,), (0,)), ((), ())), preferred_element_type=F32
+    ).astype(BF)
+    wide = jnp.dot(hot, in_row, preferred_element_type=F32)
+    same = day(0, (size, LANES), 0) == iota((size, LANES), 1) % days
+    in_out[:, :LANES] = jnp.where(same, wide, 0.0).astype(BF)
+    same = day(0, (size, days), 0) == iota((size, days), 1)
+    b_high, b_low = halves(column[:, layers : layers + 1])
+    for at, part in ((LANES, b_high), (LANES + days, b_low)):
+        in_out[:, at : at + days] = jnp.where(
+            same, jnp.broadcast_to(part.astype(F32), (size, days)), 0.0
+        ).astype(BF)
+    out_row = nt(jnp.broadcast_to(out_ref[...], (8, channels)), hot)
+    same = iota((days, size), 0) == day(0, (days, size), 1)
+    out_out[...] = jnp.where(same, jnp.broadcast_to(out_row[0:1], (days, size)), 0.0).astype(BF)
+
+    bands, tiles = lax.axis_size("day"), lax.axis_size("tile")
+    band_at, tile_at = lax.axis_index("day"), lax.axis_index("tile")
+    cols, rows = width - 2 * HALO, 16
+    for b in range(expand_out.shape[0]):
+        row, q = place_of(b, width, (LANES, LANES))
+        side = jnp.where(q < HALO, 1, jnp.where(q >= cols + HALO, 2, 0))
+        hit = (24 * side + row == iota((LANES, LANES), 0)) & (row < rows + 2 * HALO)
+        expand_out[b] = jnp.where(hit, 1.0, 0.0).astype(BF)
+        row, q = place_of(b, width, (1, LANES))
+        low_r = jnp.where(band_at == 0, HALO, 0)
+        high_r = jnp.where(band_at == bands - 1, rows + HALO, rows + 2 * HALO)
+        low_q = jnp.where(tile_at == 0, HALO, 0)
+        high_q = jnp.where(tile_at == tiles - 1, cols + HALO, cols + 2 * HALO)
+        inside = (row >= low_r) & (row < high_r) & (q >= low_q) & (q < high_q)
+        valid_out[b : b + 1] = jnp.where(inside, 1.0, 0.0)
 
 
 def chunked(low, high, step, fn):
@@ -141,33 +261,27 @@
     sources,
     arrived_ref,
     land_ref,
-    valid_ref,
+    land_left_ref,
+    land_right_ref,
     own_land_ref,
-    expand_ref,
-    in_ref,
-    first_ref,
-    rest_ref,
-    bias_ref,
-    out_w_ref,
     out_b_ref,
-    banded_ref,
-    out_ref,
-    x_ref,
-    v_ref,
-    taps,
-    y_ref,
-    sem,
+    *refs,
 ):
+    given, out_ref, x_ref, v_ref, y_ref = refs[:8], refs[8], refs[9], refs[10], refs[11]
+    held, taps_sem, sem = refs[12:20], refs[20], refs[21]
+    banded_ref, first_ref, rest_ref, bias_ref, in_ref, out_w_ref, expand_ref, valid_ref = held
+    copies = [pltpu.make_async_copy(given[i], held[i], sem.at[i]) for i in range(1, 8)]
+    for copy in copies[::-1]:
+        copy.start()
+    fetch = [
+        pltpu.make_async_copy(given[0].at[l], banded_ref.at[l], taps_sem.at[l]) for l in range(banded_ref.shape[0])
+    ]
+    for copy in fetch:
+        copy.start()
     channels = banded_ref.shape[1]
     layers = banded_ref.shape[0]
     width = LANES + 2 * HALO
     rows_in = 24
-
-    def fetch(l):
-        return pltpu.make_async_copy(banded_ref.at[l], taps.at[l % 2], sem.at[l % 2])
-
-    fetch(0).start()
-    fetch(1).start()
 
     tail = arrived_ref[:, 96:104, :].astype(F32).reshape(8 * sources, LANES).astype(BF)
     pick_r, pick_c = iota((7 * sources, 8 * sources), 0), iota((7 * sources, 8 * sources), 1)
@@ -230,11 +344,28 @@
         edge = edges[0] if b <= 16 else edges[1]
         return jnp.where(lane < start - 8, before_v, jnp.where(lane < start, edge, now_v))
 
+    land, land_left, land_right = (
+        pltpu.roll(
+            jnp.concatenate([ref[...].astype(F32), jnp.zeros((LANES - rows_in, LANES), F32)], 0), 4, 1, stride=8, stride_axis=0
+        )
+        for ref in (land_ref, land_left_ref, land_right_ref)
+    )
+    lane1 = iota((1, LANES), 1)
+
+    def land_block(b):
+        now, start = (b, 8 * b + 4) if b <= 15 else ((b - 1, 8 * b - 132) if b >= 17 else (16, 132))
+        pick = lambda a, r: a[r : r + 1] if 0 <= r < rows_in else jnp.zeros((1, LANES), F32)
+        value = jnp.where(lane1 < start - 4, pick(land_right, now - 1), pick(land_left, now))
+        value = jnp.where(lane1 < start - 8, pick(land, now - 1), value)
+        return jnp.where(lane1 < start, value, pick(land, now))
+
+    for copy in copies:
+        copy.wait()
     for j in range(13):
         pair = []
         for b in (2 * j, 2 * j + 1):
             keep = jnp.dot(cover, expand_ref[b], preferred_element_type=F32)
-            pair.append((jnp.concatenate([flat_block(b), keep, keep], 0) * land_ref[b : b + 1]).astype(BF))
+            pair.append((jnp.concatenate([flat_block(b), keep, keep], 0) * land_block(b)).astype(BF))
         got = jnp.dot(in_ref[...], jnp.concatenate(pair, 1), preferred_element_type=F32).astype(BF)
         x_ref[2 * j] = got[:, :LANES]
         x_ref[2 * j + 1] = got[:, LANES:]
@@ -251,7 +382,7 @@
             if l == 0:
                 acc = jnp.dot(first_ref[half], both, preferred_element_type=F32)
             else:
-                acc = jnp.dot(rest_ref[l - 1, p], both[half], preferred_element_type=F32)
+                acc = jnp.dot(rest_ref[l - 1], both[half], preferred_element_type=F32)
             h = acc + jnp.concatenate([bias[half], bias[half]], 1)
             v = ((h + h * jnp.tanh(h)) * ok).astype(BF)
             v_ref[2 * j + 2, half] = v[:, :LANES]
@@ -267,7 +398,10 @@
             ],
             0,
         )
-        acc = jnp.dot(lhs, taps[l % 2, c], preferred_element_type=F32)
+        t = [jnp.zeros((LANES, LANES), BF)] + [banded_ref[l, c, i] for i in range(5)]
+        t = t + [t[0]]
+        rhs = jnp.concatenate([jnp.concatenate([t[a + 1], t[a]], 1) for a in range(6)], 0)
+        acc = jnp.dot(lhs, rhs, preferred_element_type=F32)
         at = 0
         for j in range(low, high):
             for rows in groups:
@@ -280,10 +414,8 @@
         low_v, high_v = l * width // 256, -(-(rows_in - l) * width // 256)
         low_x, high_x = (l + 1) * width // 256, -(-(rows_in - l - 1) * width // 256)
         chunked(low_v, high_v, 4, functools.partial(mix, l))
-        fetch(l).wait()
+        fetch[l].wait()
         chunked(0, channels, 4, functools.partial(stencil, l, low_x, high_x))
-        if l + 2 < layers:
-            fetch(l + 2).start()
 
     for j in range(2, 11):
         got = jnp.dot(
@@ -298,7 +430,7 @@
         value = pltpu.roll(y_ref[block], back, 1) if back else y_ref[block]
         if start:
             value = jnp.where(lane_d < LANES - start, value, pltpu.roll(y_ref[block + 1], back, 1))
-        out_ref[:, r, :] = (value + out_b_ref[0]) * own_land_ref[r : r + 1]
+        out_ref[:, r, :] = (value + out_b_ref[0]) * own_land_ref[r : r + 1].astype(F32)
 
 
 def local(
@@ -323,83 +455,65 @@
     layers = mix_weight.shape[0]
     sources = bands * tiles
     width = cols + 2 * HALO
-    tall = rows + 2 * HALO
-    band_at, tile_at = lax.axis_index("day"), lax.axis_index("tile")
     slots = scene_rows.shape[3]
     n_block = 26
 
-    notes = jnp.concatenate([granule_list.reshape(-1), band_at.reshape(1).astype(jnp.int32)])
+    notes = jnp.transpose(granule_list.reshape(days_here, bands, 3), (2, 1, 0))
     granules = days_here * bands
     outgoing = pl.pallas_call(
         functools.partial(pack_kernel, tiles, bands, days_here),
         out_shape=jax.ShapeDtypeStruct((sources, 104, cols), BF),
-        in_specs=[VMEM, SMEM],
+        in_specs=[HBM, SMEM],
         out_specs=VMEM,
         scratch_shapes=[
+            pltpu.VMEM((variables, slots, cols), BF),
             pltpu.VMEM((variables, slots + 32, cols), F32),
             pltpu.VMEM((bands, 64, cols), F32),
             pltpu.VMEM((granules, 64, cols), BF),
             pltpu.VMEM((granules, 8, cols), F32),
             pltpu.VMEM(((bands + 2) * (tiles + 2), 8, cols), F32),
+            pltpu.SemaphoreType.DMA((variables,)),
         ],
-        compiler_params=pltpu.CompilerParams(vmem_limit_bytes=32 * 2**20),
+        compiler_params=pltpu.CompilerParams(vmem_limit_bytes=60 * 2**20),
         name="pack",
     )(scene_rows.reshape(variables, slots, cols), notes)
+
+    size = channels * days
+    shape = lambda *dims, dtype=BF: jax.ShapeDtypeStruct(dims, dtype)
+    land_mask, time_taps, outgoing = lax.optimization_barrier((land_mask, time_taps, outgoing))
+    params = (
+        jnp.transpose(space_taps, (2, 0, 1)),
+        jnp.transpose(time_taps, (2, 0, 1)),
+        mix_weight,
+        mix_bias,
+        in_weight.T,
+        obs_bias.reshape(1, channels),
+        out_weight.reshape(1, channels),
+    )
+    made = (
+        shape(layers, channels, 5, LANES, LANES),
+        shape(size, size),
+        shape(layers - 1, size // 2, size // 2),
+        shape(layers, size, LANES, dtype=F32),
+        shape(size, (variables + 2) * days),
+        shape(days, size),
+        shape(n_block, LANES, LANES),
+        shape(n_block, LANES, dtype=F32),
+    )
+    weights = pl.pallas_call(
+        functools.partial(weights_kernel, width),
+        out_shape=made,
+        in_specs=[HBM] * 7,
+        out_specs=(HBM,) * 8,
+        scratch_shapes=[pltpu.SMEM(params[0].shape, F32)]
+        + [pltpu.VMEM(a.shape, a.dtype) for a in params[1:]]
+        + [pltpu.VMEM(a.shape, a.dtype) for a in made]
+        + [pltpu.SemaphoreType.DMA((8,))],
+        compiler_params=pltpu.CompilerParams(vmem_limit_bytes=60 * 2**20),
+        cost_estimate=pl.CostEstimate(flops=2 * 10**9, bytes_accessed=24 * 2**20, transcendentals=0),
+        name="weights",
+    )(*params)
     arrived = lax.all_to_all(outgoing, ("day", "tile"), split_axis=0, concat_axis=0, tiled=True)
-
-    half = days // 2
-    order = jnp.arange(2 * channels * half)
-    ch_of = (order // half) % channels
-    day_of = 2 * (order % half) + order // (channels * half)
-    gap = day_of[None, :] - day_of[:, None]
-    pair = [mix_weight[l].astype(F32)[ch_of][:, ch_of] for l in range(0)]
-    del pair
-
-    def day_matrix(l, n_par):
-        spacing = 2**l
-        w = 0.5 * mix_weight[l].astype(F32)[:, :, None] * time_taps[l][None, :, :]
-        d = 2 * jnp.arange(half)[None, :] + jnp.arange(2)[:, None]
-        diff = d[None, None, :, :] - d[:, :, None, None]
-        hit = jnp.stack([(diff == (k - 1) * spacing).astype(F32) for k in range(3)], -1)
-        full = sum(
-            w[None, :, None, None, :, None, k] * hit[:, None, :, :, None, :, k] for k in range(3)
-        )
-        return full.astype(BF)
-
-    first = day_matrix(0, 2).reshape(channels * days, channels * days)
-    rest = jnp.stack(
-        [
-            jnp.stack(
-                [
-                    day_matrix(l, 2)[p, :, :, p].reshape(channels * half, channels * half)
-                    for p in range(2)
-                ]
-            )
-            for l in range(1, layers)
-        ]
-    )
-    by_row = lambda a: jnp.broadcast_to(a[..., None, :, None], a.shape[:-1] + (2, channels, half)).reshape(
-        a.shape[:-1] + (channels * days,)
-    )
-    bias = jnp.broadcast_to(0.5 * by_row(mix_bias)[..., None], (layers, channels * days, LANES))
-    same_day = (day_of[:, None] == jnp.arange(days)[None, :]).astype(F32)
-    bias_hi = obs_bias.astype(BF).astype(F32)
-    in_cols = [by_row(in_weight[:, v].astype(F32))[:, None] * same_day for v in range(variables)]
-    in_cols += [by_row(b)[:, None] * same_day for b in (bias_hi, obs_bias - bias_hi)]
-    in_full = jnp.concatenate(in_cols, 1).astype(BF)
-    out_full = (by_row(out_weight.astype(F32))[:, None] * same_day).T.astype(BF)
-
-    banded = pl.pallas_call(
-        functools.partial(banded_kernel, width),
-        grid=(layers * channels,),
-        out_shape=jax.ShapeDtypeStruct((layers * channels, 768, 256), BF),
-        in_specs=[SMEM],
-        out_specs=pl.BlockSpec((1, 768, 256), lambda i: (i, 0, 0)),
-        cost_estimate=pl.CostEstimate(
-            flops=64 * 768 * 256 * 8, bytes_accessed=64 * 768 * 256 * 2, transcendentals=0
-        ),
-        name="banded",
-    )(space_taps.reshape(-1)).reshape(layers, channels, 768, 256)
 
     forward = lambda n: [(i, i + 1) for i in range(n - 1)]
     backward = lambda n: [(i + 1, i) for i in range(n - 1)]
@@ -412,51 +526,31 @@
         ],
         0,
     )
-    land = jnp.concatenate(
-        [
-            lax.ppermute(land[:, cols - HALO :], "tile", forward(tiles)),
-            land,
-            lax.ppermute(land[:, :HALO], "tile", backward(tiles)),
-        ],
-        1,
-    ).astype(F32)
-    r, q = jnp.arange(tall)[:, None], jnp.arange(width)[None, :]
-    outside = ((r < HALO) & (band_at == 0)) | ((r >= rows + HALO) & (band_at == bands - 1))
-    outside = outside | ((q < HALO) & (tile_at == 0)) | ((q >= cols + HALO) & (tile_at == tiles - 1))
-    valid = jnp.where(outside, 0.0, 1.0)
-    flat = lambda a: jnp.pad(a.reshape(-1), (0, n_block * LANES - tall * width)).reshape(n_block, LANES)
-    position = jnp.arange(n_block * LANES).reshape(n_block, 1, LANES)
-    region = jnp.where(position % width < HALO, 1, jnp.where(position % width >= cols + HALO, 2, 0))
-    slot = jnp.where(position < tall * width, 24 * region + position // width, -1)
-    expand = (slot == jnp.arange(LANES)[None, :, None]).astype(BF)
+    land_left = lax.ppermute(land, "tile", forward(tiles))
+    land_right = lax.ppermute(land, "tile", backward(tiles))
 
     return pl.pallas_call(
         functools.partial(main_kernel, sources),
         out_shape=jax.ShapeDtypeStruct((days, rows, cols), F32),
-        in_specs=[VMEM] * 10 + [SMEM, ANY],
+        in_specs=[VMEM] * 5 + [SMEM] + [HBM] * 8,
         out_specs=VMEM,
         scratch_shapes=[
             pltpu.VMEM((n_block, channels * days, LANES), BF),
             pltpu.VMEM((n_block + 4, channels * days, LANES), BF),
-            pltpu.VMEM((2, channels, 768, 256), BF),
             pltpu.VMEM((n_block, days, LANES), F32),
-            pltpu.SemaphoreType.DMA((2,)),
-        ],
-        compiler_params=pltpu.CompilerParams(vmem_limit_bytes=44 * 2**20),
+        ]
+        + [pltpu.VMEM(a.shape, a.dtype) for a in made]
+        + [pltpu.SemaphoreType.DMA((layers,)), pltpu.SemaphoreType.DMA((8,))],
+        compiler_params=pltpu.CompilerParams(vmem_limit_bytes=60 * 2**20),
         name="blocks",
     )(
         arrived,
-        flat(land),
-        flat(valid),
-        land_mask.astype(F32),
-        expand,
-        in_full,
-        first,
-        rest,
-        bias,
-        out_full,
+        land,
+        land_left,
+        land_right,
+        land_mask,
         out_bias,
-        banded,
+        *weights,
     )
 
 

time: 144 us -> 70.2 us (0.49); the launches traced: 142 us -> 69.7 us
  local copies, waits for them, and re-layouts: 39.7 us -> 0.96 us
  other arithmetic: 23.9 us -> 0.71 us
  Pallas kernels: 57.9 us -> 45.7 us
  waiting for transfers between devices: 1.6 us -> 3.33 us
    pallas_call x1, Pallas kernels: 27.5 us -> 9.54 us  [local(): pl.pallas_call(functools.partial(weights_kernel, width), out_shape=made,...]
    convert_element_type x7 -> x1, other arithmetic: 15.9 us -> 0.7 us  [local(): land = land_mask.astype(BF)]
    convert_element_type x4 -> x0, local copies, waits for them, and re-layouts: 14.3 us -> none  [the longest x2 12.8 us: day_matrix(): return full.astype(BF)]
    another operation x6 -> x0, local copies, waits for them, and re-layouts: 6.6 us -> none  [local(): jnp.stack([day_matrix(l, 2)[p, :, :, p].reshape(channels * half, channels...]
    slice x5 -> x0, local copies, waits for them, and re-layouts: 5.22 us -> none  [the longest x3 4.29 us: local(): day_matrix(l, 2)[p, :, :, p].reshape(channels * half, channels * half)]
    pallas_call x1, Pallas kernels: 27.1 us -> 32.1 us  [local(): pl.pallas_call(functools.partial(main_kernel, sources), out_shape=jax.Sha...]
    broadcast_in_dim x9 -> x0, local copies, waits for them, and re-layouts: 4.71 us -> none  [the longest x8 4.38 us: local(): jnp.broadcast_to(a[..., None, :, None], a.shape[:-1] + (2, channels, half))]
    ppermute x1, waiting for transfers between devices: 0.01 us -> 3.32 us  [local(): lax.ppermute(land[:HALO], 'day', backward(bands))]
  transfers between devices with their start and end apart: 5 -> 5, of which waited for: 1 -> 1; matrix products, arithmetic and copies ran while one was open for 43% -> 1% of each run, Pallas kernels for 22% -> 14%
where the time goes in v1:
time: 70.2 us; the launch traced here: 69.7 us
  Pallas kernels  45.7 us (65%)
  starting transfers between devices  18.2 us (26%)
  waiting for transfers between devices  3.33 us (5%)
  local copies, waits for them, and re-layouts  0.96 us (1%)
  between operations  0.78 us (1%)
  other arithmetic  0.71 us (1%)
    pallas_call x1, Pallas kernels, local(): pl.pallas_call(functools.partial(main_kernel, sources), out_shape=jax.Sha...  32.1 us
    pallas_call x1, Pallas kernels, local(): pl.pallas_call(functools.partial(weights_kernel, width), out_shape=made,...  9.54 us
    all_to_all x1, starting transfers between devices, local(): lax.all_to_all(outgoing, ('day', 'tile'), split_axis=0, concat_axis=0, ti...  6.23 us
    pallas_call x1, Pallas kernels, local(): pl.pallas_call(functools.partial(pack_kernel, tiles, bands, days_here), o...  4.07 us
    ppermute x1, starting transfers between devices, local(): land_right = lax.ppermute(land, 'tile', backward(tiles))  3.4 us
    ppermute x1, waiting for transfers between devices, local(): lax.ppermute(land[:HALO], 'day', backward(bands))  3.32 us
    ppermute x1, starting transfers between devices, local(): land_left = lax.ppermute(land, 'tile', forward(tiles))  3.28 us
    ppermute x1, starting transfers between devices, local(): lax.ppermute(land[rows - HALO:], 'day', forward(bands))  3.09 us
  transfers between devices with their start and end apart: 5, of which 1 were waited for; matrix products, arithmetic and copies ran while one was open for 1% of the time, Pallas kernels for 14%

profile of v1, /device:TPU:19, one launch (start us, length us, event | category | flops | bytes accessed | tf_op | source)
XLA Modules:
  0.0 69.7 jit_solution(9797206502171856763)
XLA Ops:
  0.0 4.1 %pack.1 = bf16[32,104,128]{2,1,0:T(8,128)(2,1)} custom-call(bf16[4,512,128]{2,1,0:T(8,128)(2,1)} %bitcast.9, s32[3,4,8]{2,1,0:T(4,128)} %bitcast.10), custom_call_target="tpu_custom_call" | custom-call | tf_op jit(solution)/shard_map/pack/pallas_call | solution.py:463
  4.1 6.2 %all-to-all-start = ((bf16[32,104,128]{2,1,0:T(8,128)(2,1)}), bf16[32,104,128]{2,1,0:T(8,128)(2,1)S(1)}, u32[]{:S(2)}, u32[]{:S(2)}) async-start(bf16[32,104,128]{2,1,0:T(8,128)(2,1)} %pack.1), calls=%async_computation | async-start | bytes 1703936 | tf_op jit(solution)/shard_map/all_to_all | solution.py:516
  10.3 0.7 %convert_element_type.3 = bf16[16,128]{1,0:T(8,128)(2,1)S(1)} convert(s32[16,128]{1,0:T(8,128)} %own_land_ref) | non-fusion elementwise | flops 2048 | bytes 12288 | tf_op jit(solution)/shard_map/convert_element_type | solution.py:520
  11.0 3.1 %collective-permute-start = (bf16[4,128]{1,0:T(4,128)(2,1)S(1)}, bf16[4,128]{1,0:T(4,128)(2,1)S(1)}, u32[]{:S(2)}, u32[]{:S(2)}) collective-permute-start(bf16[4,128]{1,0:T(4,128)(2,1)S(1)} %get-tuple-element.27), channel_id=1, source_target_pairs={{0,8},{8,16},{16,24},{1,9},{9,17},{17,25},{2,10},{10,18},{18,26},{... | collective-permute-start | bytes 3080 | tf_op jit(solution)/shard_map/ppermute | solution.py:523
  14.1 2.2 %collective-permute-start.1 = (bf16[4,128]{1,0:T(4,128)(2,1)S(1)}, bf16[4,128]{1,0:T(4,128)(2,1)S(1)}, u32[]{:S(2)}, u32[]{:S(2)}) collective-permute-start(bf16[4,128]{1,0:T(4,128)(2,1)S(1)} %get-tuple-element.28), channel_id=1, source_target_pairs={{8,0},{16,8},{24,16},{9,1},{17,9},{25,17},{10,2},{18,10},{26,18},{... | collective-permute-start | bytes 3080 | tf_op jit(solution)/shard_map/ppermute | solution.py:525
  16.3 0.0 collective-permute-done
  16.3 3.3 %collective-permute-done.1 = bf16[4,128]{1,0:T(4,128)(2,1)S(1)} collective-permute-done((bf16[4,128]{1,0:T(4,128)(2,1)S(1)}, bf16[4,128]{1,0:T(4,128)(2,1)S(1)}, u32[]{:S(2)}, u32[]{:S(2)}) %collective-permute-start.1) | collective-permute-done | bytes 1056 | tf_op jit(solution)/shard_map/ppermute | solution.py:525
  19.6 0.0 copy-start.1
  19.7 3.4 %collective-permute-start.3 = (bf16[24,128]{1,0:T(8,128)(2,1)S(1)}, bf16[24,128]{1,0:T(8,128)(2,1)S(1)}, u32[]{:S(2)}, u32[]{:S(2)}) collective-permute-start(bf16[24,128]{1,0:T(8,128)(2,1)S(1)} %pad_maximum_fusion.land_ref), channel_id=1, source_target_pairs={{1,0},{2,1},{3,2},{4,3},{5,4},{6,5},{7,6},{9,8},{10,9},{11,10},{12... | collective-permute-start | bytes 18440 | tf_op jit(solution)/shard_map/ppermute | solution.py:530
  23.1 3.3 %collective-permute-start.2 = (bf16[24,128]{1,0:T(8,128)(2,1)S(1)}, bf16[24,128]{1,0:T(8,128)(2,1)S(1)}, u32[]{:S(2)}, u32[]{:S(2)}) collective-permute-start(bf16[24,128]{1,0:T(8,128)(2,1)S(1)} %pad_maximum_fusion.land_ref), channel_id=1, source_target_pairs={{0,1},{1,2},{2,3},{3,4},{4,5},{5,6},{6,7},{8,9},{9,10},{10,11},{11... | collective-permute-start | bytes 18440 | tf_op jit(solution)/shard_map/ppermute | solution.py:529
  26.4 9.5 %weights.1 = (bf16[4,16,5,128,128]{4,3,2,1,0:T(8,128)(2,1)}, bf16[512,512]{1,0:T(8,128)(2,1)}, bf16[3,256,256]{2,1,0:T(8,128)(2,1)}, f32[4,512,128]{2,1,0:T(8,12...) custom-call(f32[9,4,16]{2,1,0:T(4,128)} %bitcast.11, ...), custom_call_target="tpu_custom_call" | custom-call | flops 2000000000 | bytes 25165824 | tf_op jit(solution)/shard_map/weights/pallas_call | solution.py:503
  36.5 0.0 collective-permute-done.3.land_right_ref
  36.6 0.0 copy-start.2
  36.6 0.0 collective-permute-done.2.land_left_ref
  36.6 0.0 copy-start.3
  36.6 0.0 all-to-all-done.arrived_ref
  36.6 0.0 copy-start
  36.6 0.0 copy-done.1
  36.6 0.5 copy-done.2
  37.2 0.0 copy-done.3
  37.2 0.4 copy-done
  37.6 32.1 %blocks.1 = f32[32,16,128]{2,1,0:T(8,128)} custom-call(bf16[32,104,128]{2,1,0:T(8,128)(2,1)} %copy-done, bf16[24,128]{1,0:T(8,128)(2,1)} %copy-done.1, bf16[24,128]{1,0:T(8,128)(2,1)} %copy-done.3, bf16[24,128]{1,0:T(8,128)(2,1)} %copy-done.2, s32[16,128]{1,0:T(8,128)} %own_land_ref, f32[1]{0:T(128)S(6)} %copy.12.out_b_ref, ...), custom_call_target="tpu_custom_call" | custom-call | tf_op jit(solution)/shard_map/blocks/pallas_call | solution.py:532
  (2 shorter events, 0.0 us)
Async XLA Ops:
  4.1 32.5 %all-to-all-start = ((bf16[32,104,128]{2,1,0:T(8,128)(2,1)}), bf16[32,104,128]{2,1,0:T(8,128)(2,1)S(1)}, u32[]{:S(2)}, u32[]{:S(2)}) async-start(bf16[32,104,128]{2,1,0:T(8,128)(2,1)} %pack.1), calls=%async_computation | async-start | bytes 1703936 | tf_op jit(solution)/shard_map/all_to_all | solution.py:516
  11.0 5.3 %collective-permute-start = (bf16[4,128]{1,0:T(4,128)(2,1)S(1)}, bf16[4,128]{1,0:T(4,128)(2,1)S(1)}, u32[]{:S(2)}, u32[]{:S(2)}) collective-permute-start(bf16[4,128]{1,0:T(4,128)(2,1)S(1)} %get-tuple-element.27), channel_id=1, source_target_pairs={{0,8},{8,16},{16,24},{1,9},{9,17},{17,25},{2,10},{10,18},{18,26},{... | collective-permute-start | bytes 3080 | tf_op jit(solution)/shard_map/ppermute | solution.py:523
  14.1 5.5 %collective-permute-start.1 = (bf16[4,128]{1,0:T(4,128)(2,1)S(1)}, bf16[4,128]{1,0:T(4,128)(2,1)S(1)}, u32[]{:S(2)}, u32[]{:S(2)}) collective-permute-start(bf16[4,128]{1,0:T(4,128)(2,1)S(1)} %get-tuple-element.28), channel_id=1, source_target_pairs={{8,0},{16,8},{24,16},{9,1},{17,9},{25,17},{10,2},{18,10},{26,18},{... | collective-permute-start | bytes 3080 | tf_op jit(solution)/shard_map/ppermute | solution.py:525
  19.6 17.0 %copy-start.1 = (bf16[24,128]{1,0:T(8,128)(2,1)}, bf16[24,128]{1,0:T(8,128)(2,1)S(1)}, u32[]{:S(2)}) copy-start(bf16[24,128]{1,0:T(8,128)(2,1)S(1)} %pad_maximum_fusion.land_ref) | copy-start | bytes 18436
  19.7 16.9 %collective-permute-start.3 = (bf16[24,128]{1,0:T(8,128)(2,1)S(1)}, bf16[24,128]{1,0:T(8,128)(2,1)S(1)}, u32[]{:S(2)}, u32[]{:S(2)}) collective-permute-start(bf16[24,128]{1,0:T(8,128)(2,1)S(1)} %pad_maximum_fusion.land_ref), channel_id=1, source_target_pairs={{1,0},{2,1},{3,2},{4,3},{5,4},{6,5},{7,6},{9,8},{10,9},{11,10},{12... | collective-permute-start | bytes 18440 | tf_op jit(solution)/shard_map/ppermute | solution.py:530
  23.1 13.5 %collective-permute-start.2 = (bf16[24,128]{1,0:T(8,128)(2,1)S(1)}, bf16[24,128]{1,0:T(8,128)(2,1)S(1)}, u32[]{:S(2)}, u32[]{:S(2)}) collective-permute-start(bf16[24,128]{1,0:T(8,128)(2,1)S(1)} %pad_maximum_fusion.land_ref), channel_id=1, source_target_pairs={{0,1},{1,2},{2,3},{3,4},{4,5},{5,6},{6,7},{8,9},{9,10},{10,11},{11... | collective-permute-start | bytes 18440 | tf_op jit(solution)/shard_map/ppermute | solution.py:529
  36.6 0.6 copy-start.2
  36.6 0.6 copy-start.3
  36.6 1.0 %copy-start = (bf16[32,104,128]{2,1,0:T(8,128)(2,1)}, bf16[32,104,128]{2,1,0:T(8,128)(2,1)S(1)}, u32[]{:S(2)}) copy-start(bf16[32,104,128]{2,1,0:T(8,128)(2,1)S(1)} %all-to-all-done.arrived_ref) | copy-start | bytes 2555908

commit v2 on v1

--- a/solution.py
+++ b/solution.py
@@ -243,20 +243,6 @@
         valid_out[b : b + 1] = jnp.where(inside, 1.0, 0.0)
 
 
-def chunked(low, high, step, fn):
-    count = (high - low) // step
-    spare = (high - low) - count * step
-    for i in range(low, low + spare):
-        fn(i)
-
-    def body(i, c):
-        for u in range(step):
-            fn(low + spare + i * step + u)
-        return c
-
-    lax.fori_loop(0, count, body, 0)
-
-
 def main_kernel(
     sources,
     arrived_ref,
@@ -276,8 +262,6 @@
     fetch = [
         pltpu.make_async_copy(given[0].at[l], banded_ref.at[l], taps_sem.at[l]) for l in range(banded_ref.shape[0])
     ]
-    for copy in fetch:
-        copy.start()
     channels = banded_ref.shape[1]
     layers = banded_ref.shape[0]
     width = LANES + 2 * HALO
@@ -326,10 +310,16 @@
     edges = [jnp.concatenate([packed[v][h] for v in range(4)], 0) for h in range(2)]
 
     rolled = []
-    for p in range(12):
+    pairs = []
+    for p in range(0, 12, 2):
         band = 0 if p < 2 else (2 if p >= 10 else 1)
-        rows = arrived_ref[:, 8 * p : 8 * p + 8, :].astype(F32).reshape(8 * sources, LANES).astype(BF)
-        got = jnp.dot(perms[band], rows, preferred_element_type=F32)
+        rows = [
+            arrived_ref[:, 8 * i : 8 * i + 8, :].astype(F32).reshape(8 * sources, LANES).astype(BF)
+            for i in (p, p + 1)
+        ]
+        both = jnp.dot(perms[band], jnp.concatenate(rows, 1), preferred_element_type=F32)
+        pairs += [both[:, :LANES], both[:, LANES:]]
+    for p, got in enumerate(pairs):
         for r2 in range(2):
             row = 2 * p + r2
             rolled.append(pltpu.roll(got[128 * r2 : 128 * r2 + 128], (8 * row + 4) % LANES, 1))
@@ -361,6 +351,8 @@
 
     for copy in copies:
         copy.wait()
+    for copy in fetch:
+        copy.start()
     for j in range(13):
         pair = []
         for b in (2 * j, 2 * j + 1):
@@ -375,7 +367,7 @@
 
     def mix(l, j):
         both = jnp.concatenate([x_ref[2 * j], x_ref[2 * j + 1]], 1)
-        ok = jnp.concatenate([valid_ref[pl.ds(2 * j, 1)], valid_ref[pl.ds(2 * j + 1, 1)]], 1)
+        ok = jnp.concatenate([valid_ref[2 * j : 2 * j + 1], valid_ref[2 * j + 1 : 2 * j + 2]], 1)
         bias = bias_ref[l]
         for p in range(2):
             half = slice(256 * p, 256 * p + 256)
@@ -389,7 +381,7 @@
             v_ref[2 * j + 3, half] = v[:, LANES:]
 
     def stencil(l, low, high, c):
-        groups = [pl.ds(pl.multiple_of(c * 16 + 256 * p, 16), 16) for p in range(2)]
+        groups = [slice(c * 16 + 256 * p, c * 16 + 256 * p + 16) for p in range(2)]
         lhs = jnp.concatenate(
             [
                 jnp.concatenate([v_ref[2 * j + b, rows] for b in range(6)], 1)
@@ -413,9 +405,11 @@
     for l in range(layers):
         low_v, high_v = l * width // 256, -(-(rows_in - l) * width // 256)
         low_x, high_x = (l + 1) * width // 256, -(-(rows_in - l - 1) * width // 256)
-        chunked(low_v, high_v, 4, functools.partial(mix, l))
+        for j in range(low_v, high_v):
+            mix(l, j)
         fetch[l].wait()
-        chunked(0, channels, 4, functools.partial(stencil, l, low_x, high_x))
+        for c in range(channels):
+            stencil(l, low_x, high_x, c)
 
     for j in range(2, 11):
         got = jnp.dot(

time: 70.2 us -> 61 us (0.87)
  Pallas kernels: 45.7 us -> 36.4 us
    pallas_call x1, Pallas kernels: 32.1 us -> 22.8 us  [local(): pl.pallas_call(functools.partial(main_kernel, sources), out_shape=jax.Sha...]
  transfers between devices with their start and end apart: 5 -> 5, of which waited for: 1 -> 1; matrix products, arithmetic and copies ran while one was open for 1% -> 1% of each run, Pallas kernels for 14% -> 16%
where the time goes in v2:
time: 61 us; the launch traced here: 60.5 us
  Pallas kernels  36.4 us (60%)
  starting transfers between devices  18.2 us (30%)
  waiting for transfers between devices  3.33 us (5%)
  local copies, waits for them, and re-layouts  0.96 us (2%)
  between operations  0.94 us (2%)
  other arithmetic  0.71 us (1%)
    pallas_call x1, Pallas kernels, local(): pl.pallas_call(functools.partial(main_kernel, sources), out_shape=jax.Sha...  22.8 us
    pallas_call x1, Pallas kernels, local(): pl.pallas_call(functools.partial(weights_kernel, width), out_shape=made,...  9.54 us
    all_to_all x1, starting transfers between devices, local(): lax.all_to_all(outgoing, ('day', 'tile'), split_axis=0, concat_axis=0, ti...  6.23 us
    pallas_call x1, Pallas kernels, local(): pl.pallas_call(functools.partial(pack_kernel, tiles, bands, days_here), o...  4.06 us
    ppermute x1, starting transfers between devices, local(): land_right = lax.ppermute(land, 'tile', backward(tiles))  3.4 us
    ppermute x1, waiting for transfers between devices, local(): lax.ppermute(land[:HALO], 'day', backward(bands))  3.32 us
    ppermute x1, starting transfers between devices, local(): land_left = lax.ppermute(land, 'tile', forward(tiles))  3.28 us
    ppermute x1, starting transfers between devices, local(): lax.ppermute(land[rows - HALO:], 'day', forward(bands))  3.09 us
  transfers between devices with their start and end apart: 5, of which 1 were waited for; matrix products, arithmetic and copies ran while one was open for 1% of the time, Pallas kernels for 16%

profile of v2, /device:TPU:19, one launch (start us, length us, event | category | flops | bytes accessed | tf_op | source)
XLA Modules:
  0.0 60.5 jit_solution(10680855260588225884)
XLA Ops:
  0.0 4.1 %pack.1 = bf16[32,104,128]{2,1,0:T(8,128)(2,1)} custom-call(bf16[4,512,128]{2,1,0:T(8,128)(2,1)} %bitcast.9, s32[3,4,8]{2,1,0:T(4,128)} %bitcast.10), custom_call_target="tpu_custom_call" | custom-call | tf_op jit(solution)/shard_map/pack/pallas_call | solution.py:457
  4.1 6.2 %all-to-all-start = ((bf16[32,104,128]{2,1,0:T(8,128)(2,1)}), bf16[32,104,128]{2,1,0:T(8,128)(2,1)S(1)}, u32[]{:S(2)}, u32[]{:S(2)}) async-start(bf16[32,104,128]{2,1,0:T(8,128)(2,1)} %pack.1), calls=%async_computation | async-start | bytes 1703936 | tf_op jit(solution)/shard_map/all_to_all | solution.py:510
  10.3 0.7 %convert_element_type.3 = bf16[16,128]{1,0:T(8,128)(2,1)S(1)} convert(s32[16,128]{1,0:T(8,128)} %own_land_ref) | non-fusion elementwise | flops 2048 | bytes 12288 | tf_op jit(solution)/shard_map/convert_element_type | solution.py:514
  11.0 3.1 %collective-permute-start = (bf16[4,128]{1,0:T(4,128)(2,1)S(1)}, bf16[4,128]{1,0:T(4,128)(2,1)S(1)}, u32[]{:S(2)}, u32[]{:S(2)}) collective-permute-start(bf16[4,128]{1,0:T(4,128)(2,1)S(1)} %get-tuple-element.27), channel_id=1, source_target_pairs={{0,8},{8,16},{16,24},{1,9},{9,17},{17,25},{2,10},{10,18},{18,26},{... | collective-permute-start | bytes 3080 | tf_op jit(solution)/shard_map/ppermute | solution.py:517
  14.1 2.2 %collective-permute-start.1 = (bf16[4,128]{1,0:T(4,128)(2,1)S(1)}, bf16[4,128]{1,0:T(4,128)(2,1)S(1)}, u32[]{:S(2)}, u32[]{:S(2)}) collective-permute-start(bf16[4,128]{1,0:T(4,128)(2,1)S(1)} %get-tuple-element.28), channel_id=1, source_target_pairs={{8,0},{16,8},{24,16},{9,1},{17,9},{25,17},{10,2},{18,10},{26,18},{... | collective-permute-start | bytes 3080 | tf_op jit(solution)/shard_map/ppermute | solution.py:519
  16.3 0.0 collective-permute-done
  16.3 3.3 %collective-permute-done.1 = bf16[4,128]{1,0:T(4,128)(2,1)S(1)} collective-permute-done((bf16[4,128]{1,0:T(4,128)(2,1)S(1)}, bf16[4,128]{1,0:T(4,128)(2,1)S(1)}, u32[]{:S(2)}, u32[]{:S(2)}) %collective-permute-start.1) | collective-permute-done | bytes 1056 | tf_op jit(solution)/shard_map/ppermute | solution.py:519
  19.6 0.0 copy-start.1
  19.7 3.4 %collective-permute-start.3 = (bf16[24,128]{1,0:T(8,128)(2,1)S(1)}, bf16[24,128]{1,0:T(8,128)(2,1)S(1)}, u32[]{:S(2)}, u32[]{:S(2)}) collective-permute-start(bf16[24,128]{1,0:T(8,128)(2,1)S(1)} %pad_maximum_fusion.land_ref), channel_id=1, source_target_pairs={{1,0},{2,1},{3,2},{4,3},{5,4},{6,5},{7,6},{9,8},{10,9},{11,10},{12... | collective-permute-start | bytes 18440 | tf_op jit(solution)/shard_map/ppermute | solution.py:524
  23.1 3.3 %collective-permute-start.2 = (bf16[24,128]{1,0:T(8,128)(2,1)S(1)}, bf16[24,128]{1,0:T(8,128)(2,1)S(1)}, u32[]{:S(2)}, u32[]{:S(2)}) collective-permute-start(bf16[24,128]{1,0:T(8,128)(2,1)S(1)} %pad_maximum_fusion.land_ref), channel_id=1, source_target_pairs={{0,1},{1,2},{2,3},{3,4},{4,5},{5,6},{6,7},{8,9},{9,10},{10,11},{11... | collective-permute-start | bytes 18440 | tf_op jit(solution)/shard_map/ppermute | solution.py:523
  26.4 9.5 %weights.1 = (bf16[4,16,5,128,128]{4,3,2,1,0:T(8,128)(2,1)}, bf16[512,512]{1,0:T(8,128)(2,1)}, bf16[3,256,256]{2,1,0:T(8,128)(2,1)}, f32[4,512,128]{2,1,0:T(8,12...) custom-call(f32[9,4,16]{2,1,0:T(4,128)} %bitcast.11, ...), custom_call_target="tpu_custom_call" | custom-call | flops 2000000000 | bytes 25165824 | tf_op jit(solution)/shard_map/weights/pallas_call | solution.py:497
  36.5 0.0 collective-permute-done.3.land_right_ref
  36.6 0.0 copy-start.2
  36.6 0.0 collective-permute-done.2.land_left_ref
  36.6 0.0 copy-start.3
  36.6 0.0 all-to-all-done.arrived_ref
  36.6 0.0 copy-start
  36.6 0.0 copy-done.1
  36.6 0.5 copy-done.2
  37.2 0.0 copy-done.3
  37.2 0.4 copy-done
  37.6 22.8 %blocks.1 = f32[32,16,128]{2,1,0:T(8,128)} custom-call(bf16[32,104,128]{2,1,0:T(8,128)(2,1)} %copy-done, bf16[24,128]{1,0:T(8,128)(2,1)} %copy-done.1, bf16[24,128]{1,0:T(8,128)(2,1)} %copy-done.3, bf16[24,128]{1,0:T(8,128)(2,1)} %copy-done.2, s32[16,128]{1,0:T(8,128)} %own_land_ref, f32[1]{0:T(128)S(6)} %copy.12.out_b_ref, ...), custom_call_target="tpu_custom_call" | custom-call | tf_op jit(solution)/shard_map/blocks/pallas_call | solution.py:526
  (2 shorter events, 0.0 us)
Async XLA Ops:
  4.1 32.5 %all-to-all-start = ((bf16[32,104,128]{2,1,0:T(8,128)(2,1)}), bf16[32,104,128]{2,1,0:T(8,128)(2,1)S(1)}, u32[]{:S(2)}, u32[]{:S(2)}) async-start(bf16[32,104,128]{2,1,0:T(8,128)(2,1)} %pack.1), calls=%async_computation | async-start | bytes 1703936 | tf_op jit(solution)/shard_map/all_to_all | solution.py:510
  11.0 5.3 %collective-permute-start = (bf16[4,128]{1,0:T(4,128)(2,1)S(1)}, bf16[4,128]{1,0:T(4,128)(2,1)S(1)}, u32[]{:S(2)}, u32[]{:S(2)}) collective-permute-start(bf16[4,128]{1,0:T(4,128)(2,1)S(1)} %get-tuple-element.27), channel_id=1, source_target_pairs={{0,8},{8,16},{16,24},{1,9},{9,17},{17,25},{2,10},{10,18},{18,26},{... | collective-permute-start | bytes 3080 | tf_op jit(solution)/shard_map/ppermute | solution.py:517
  14.1 5.5 %collective-permute-start.1 = (bf16[4,128]{1,0:T(4,128)(2,1)S(1)}, bf16[4,128]{1,0:T(4,128)(2,1)S(1)}, u32[]{:S(2)}, u32[]{:S(2)}) collective-permute-start(bf16[4,128]{1,0:T(4,128)(2,1)S(1)} %get-tuple-element.28), channel_id=1, source_target_pairs={{8,0},{16,8},{24,16},{9,1},{17,9},{25,17},{10,2},{18,10},{26,18},{... | collective-permute-start | bytes 3080 | tf_op jit(solution)/shard_map/ppermute | solution.py:519
  19.6 17.0 %copy-start.1 = (bf16[24,128]{1,0:T(8,128)(2,1)}, bf16[24,128]{1,0:T(8,128)(2,1)S(1)}, u32[]{:S(2)}) copy-start(bf16[24,128]{1,0:T(8,128)(2,1)S(1)} %pad_maximum_fusion.land_ref) | copy-start | bytes 18436
  19.7 16.9 %collective-permute-start.3 = (bf16[24,128]{1,0:T(8,128)(2,1)S(1)}, bf16[24,128]{1,0:T(8,128)(2,1)S(1)}, u32[]{:S(2)}, u32[]{:S(2)}) collective-permute-start(bf16[24,128]{1,0:T(8,128)(2,1)S(1)} %pad_maximum_fusion.land_ref), channel_id=1, source_target_pairs={{1,0},{2,1},{3,2},{4,3},{5,4},{6,5},{7,6},{9,8},{10,9},{11,10},{12... | collective-permute-start | bytes 18440 | tf_op jit(solution)/shard_map/ppermute | solution.py:524
  23.1 13.5 %collective-permute-start.2 = (bf16[24,128]{1,0:T(8,128)(2,1)S(1)}, bf16[24,128]{1,0:T(8,128)(2,1)S(1)}, u32[]{:S(2)}, u32[]{:S(2)}) collective-permute-start(bf16[24,128]{1,0:T(8,128)(2,1)S(1)} %pad_maximum_fusion.land_ref), channel_id=1, source_target_pairs={{0,1},{1,2},{2,3},{3,4},{4,5},{5,6},{6,7},{8,9},{9,10},{10,11},{11... | collective-permute-start | bytes 18440 | tf_op jit(solution)/shard_map/ppermute | solution.py:523
  36.6 0.6 copy-start.2
  36.6 0.6 copy-start.3
  36.6 1.0 %copy-start = (bf16[32,104,128]{2,1,0:T(8,128)(2,1)}, bf16[32,104,128]{2,1,0:T(8,128)(2,1)S(1)}, u32[]{:S(2)}) copy-start(bf16[32,104,128]{2,1,0:T(8,128)(2,1)S(1)} %all-to-all-done.arrived_ref) | copy-start | bytes 2555908

commit v3 on v2

--- a/solution.py
+++ b/solution.py
@@ -126,7 +126,7 @@
     width,
     *refs,
 ):
-    params, results, held, made, sem = refs[:7], refs[7:15], refs[15:22], refs[22:30], refs[30]
+    params, results, held, made, sem = refs[:7], refs[7:14], refs[14:21], refs[21:28], refs[28]
     copies = [pltpu.make_async_copy(a, b, sem.at[i]) for i, (a, b) in enumerate(zip(params, held))]
     for copy in copies:
         copy.start()
@@ -155,7 +155,6 @@
     bias_out,
     in_out,
     out_out,
-    expand_out,
     valid_out,
 ):
     layers, channels = mix_ref.shape[0], mix_ref.shape[1]
@@ -200,13 +199,13 @@
         else:
             rest_out[l - 1] = value.astype(BF)
 
-    rows8 = jnp.concatenate([0.5 * mix_bias_ref[...], obs_bias_ref[...], jnp.zeros((3, channels), F32)], 0)
+    spare = jnp.zeros((LANES - layers - 1, channels), F32)
+    rows8 = jnp.concatenate([0.5 * mix_bias_ref[...], obs_bias_ref[...], spare], 0)
     high, rest = halves(rows8)
     mid, low = halves(rows8 - high.astype(F32))
     nt = lambda a, b: lax.dot_general(a, b, (((1,), (1,)), ((), ())), preferred_element_type=F32)
     column = nt(hot, high) + (nt(hot, mid) + nt(hot, low))
-    for l in range(layers):
-        bias_out[l] = jnp.broadcast_to(column[:, l : l + 1], (size, LANES))
+    bias_out[...] = column
 
     variables = in_ref.shape[0]
     repeat = (iota((variables, LANES), 1) // days == iota((variables, LANES), 0)).astype(F32).astype(BF)
@@ -229,11 +228,7 @@
     bands, tiles = lax.axis_size("day"), lax.axis_size("tile")
     band_at, tile_at = lax.axis_index("day"), lax.axis_index("tile")
     cols, rows = width - 2 * HALO, 16
-    for b in range(expand_out.shape[0]):
-        row, q = place_of(b, width, (LANES, LANES))
-        side = jnp.where(q < HALO, 1, jnp.where(q >= cols + HALO, 2, 0))
-        hit = (24 * side + row == iota((LANES, LANES), 0)) & (row < rows + 2 * HALO)
-        expand_out[b] = jnp.where(hit, 1.0, 0.0).astype(BF)
+    for b in range(valid_out.shape[0]):
         row, q = place_of(b, width, (1, LANES))
         low_r = jnp.where(band_at == 0, HALO, 0)
         high_r = jnp.where(band_at == bands - 1, rows + HALO, rows + 2 * HALO)
@@ -245,7 +240,6 @@
 
 def main_kernel(
     sources,
-    arrived_ref,
     land_ref,
     land_left_ref,
     land_right_ref,
@@ -253,20 +247,33 @@
     out_b_ref,
     *refs,
 ):
-    given, out_ref, x_ref, v_ref, y_ref = refs[:8], refs[8], refs[9], refs[10], refs[11]
-    held, taps_sem, sem = refs[12:20], refs[20], refs[21]
-    banded_ref, first_ref, rest_ref, bias_ref, in_ref, out_w_ref, expand_ref, valid_ref = held
-    copies = [pltpu.make_async_copy(given[i], held[i], sem.at[i]) for i in range(1, 8)]
-    for copy in copies[::-1]:
-        copy.start()
+    given, out_ref, x_ref, v_ref, y_ref, bias_ref = refs[:8], refs[8], refs[9], refs[10], refs[11], refs[12]
+    held, taps_sem, sem = refs[13:21], refs[21], refs[22]
+    arrived_ref, banded_ref, first_ref, rest_ref, column_ref, in_ref, out_w_ref, valid_ref = held
+    names = ("arrived", "banded", "first", "rest", "column", "in", "out", "valid")
+    copies = {
+        name: pltpu.make_async_copy(a, b, sem.at[i])
+        for i, (name, a, b) in enumerate(zip(names, given, held))
+        if name != "banded"
+    }
+    for name in ("arrived", "in", "column", "first", "valid", "rest", "out"):
+        copies[name].start()
     fetch = [
-        pltpu.make_async_copy(given[0].at[l], banded_ref.at[l], taps_sem.at[l]) for l in range(banded_ref.shape[0])
+        pltpu.make_async_copy(given[1].at[l], banded_ref.at[l], taps_sem.at[l]) for l in range(banded_ref.shape[0])
     ]
     channels = banded_ref.shape[1]
     layers = banded_ref.shape[0]
     width = LANES + 2 * HALO
     rows_in = 24
 
+    lane = iota((LANES, LANES), 1)
+
+    def expand(b):
+        row, q = place_of(b, width, (LANES, LANES))
+        side = jnp.where(q < HALO, 1, jnp.where(q >= LANES + HALO, 2, 0))
+        return jnp.where((24 * side + row == iota((LANES, LANES), 0)) & (row < rows_in), 1.0, 0.0).astype(BF)
+
+    copies["arrived"].wait()
     tail = arrived_ref[:, 96:104, :].astype(F32).reshape(8 * sources, LANES).astype(BF)
     pick_r, pick_c = iota((7 * sources, 8 * sources), 0), iota((7 * sources, 8 * sources), 1)
     pick = ((pick_c // 8 == pick_r % sources) & (pick_c % 8 == pick_r // sources)).astype(F32).astype(BF)
@@ -323,7 +330,6 @@
         for r2 in range(2):
             row = 2 * p + r2
             rolled.append(pltpu.roll(got[128 * r2 : 128 * r2 + 128], (8 * row + 4) % LANES, 1))
-    lane = iota((LANES, LANES), 1)
     zero = jnp.zeros((LANES, LANES), F32)
 
     def flat_block(b):
@@ -349,25 +355,28 @@
         value = jnp.where(lane1 < start - 8, pick(land, now - 1), value)
         return jnp.where(lane1 < start, value, pick(land, now))
 
-    for copy in copies:
-        copy.wait()
+    copies["in"].wait()
     for copy in fetch:
         copy.start()
     for j in range(13):
         pair = []
         for b in (2 * j, 2 * j + 1):
-            keep = jnp.dot(cover, expand_ref[b], preferred_element_type=F32)
+            keep = jnp.dot(cover, expand(b), preferred_element_type=F32)
             pair.append((jnp.concatenate([flat_block(b), keep, keep], 0) * land_block(b)).astype(BF))
         got = jnp.dot(in_ref[...], jnp.concatenate(pair, 1), preferred_element_type=F32).astype(BF)
         x_ref[2 * j] = got[:, :LANES]
         x_ref[2 * j + 1] = got[:, LANES:]
 
+    for name in ("column", "first", "valid"):
+        copies[name].wait()
+    for l in range(layers):
+        bias_ref[l] = jnp.broadcast_to(column_ref[:, l : l + 1], bias_ref.shape[1:])
     for b in (0, 1, 28, 29):
         v_ref[b] = jnp.zeros(v_ref.shape[1:], BF)
 
-    def mix(l, j):
-        both = jnp.concatenate([x_ref[2 * j], x_ref[2 * j + 1]], 1)
-        ok = jnp.concatenate([valid_ref[2 * j : 2 * j + 1], valid_ref[2 * j + 1 : 2 * j + 2]], 1)
+    def mix(l, b):
+        both = jnp.concatenate([x_ref[b], x_ref[b + 1]], 1)
+        ok = jnp.concatenate([valid_ref[b : b + 1], valid_ref[b + 1 : b + 2]], 1)
         bias = bias_ref[l]
         for p in range(2):
             half = slice(256 * p, 256 * p + 256)
@@ -377,15 +386,15 @@
                 acc = jnp.dot(rest_ref[l - 1], both[half], preferred_element_type=F32)
             h = acc + jnp.concatenate([bias[half], bias[half]], 1)
             v = ((h + h * jnp.tanh(h)) * ok).astype(BF)
-            v_ref[2 * j + 2, half] = v[:, :LANES]
-            v_ref[2 * j + 3, half] = v[:, LANES:]
-
-    def stencil(l, low, high, c):
+            v_ref[b + 2, half] = v[:, :LANES]
+            v_ref[b + 3, half] = v[:, LANES:]
+
+    def stencil(l, starts, c):
         groups = [slice(c * 16 + 256 * p, c * 16 + 256 * p + 16) for p in range(2)]
         lhs = jnp.concatenate(
             [
-                jnp.concatenate([v_ref[2 * j + b, rows] for b in range(6)], 1)
-                for j in range(low, high)
+                jnp.concatenate([v_ref[b + i, rows] for i in range(6)], 1)
+                for b in starts
                 for rows in groups
             ],
             0,
@@ -395,22 +404,26 @@
         rhs = jnp.concatenate([jnp.concatenate([t[a + 1], t[a]], 1) for a in range(6)], 0)
         acc = jnp.dot(lhs, rhs, preferred_element_type=F32)
         at = 0
-        for j in range(low, high):
+        for b in starts:
             for rows in groups:
                 for h in range(2):
                     part = acc[at : at + 16, LANES * h : LANES * h + LANES]
-                    x_ref[2 * j + h, rows] = (x_ref[2 * j + h, rows].astype(F32) + part).astype(BF)
+                    x_ref[b + h, rows] = (x_ref[b + h, rows].astype(F32) + part).astype(BF)
                 at += 16
 
     for l in range(layers):
-        low_v, high_v = l * width // 256, -(-(rows_in - l) * width // 256)
-        low_x, high_x = (l + 1) * width // 256, -(-(rows_in - l - 1) * width // 256)
-        for j in range(low_v, high_v):
-            mix(l, j)
+        pairs_v, pairs_x = (
+            range(low * width // LANES, -(-(rows_in - low) * width // LANES), 2) for low in (l, l + 1)
+        )
+        if l == 1:
+            copies["rest"].wait()
+        for b in pairs_v:
+            mix(l, b)
         fetch[l].wait()
         for c in range(channels):
-            stencil(l, low_x, high_x, c)
-
+            stencil(l, pairs_x, c)
+
+    copies["out"].wait()
     for j in range(2, 11):
         got = jnp.dot(
             out_w_ref[...], jnp.concatenate([x_ref[2 * j], x_ref[2 * j + 1]], 1), preferred_element_type=F32
@@ -488,17 +501,16 @@
         shape(layers, channels, 5, LANES, LANES),
         shape(size, size),
         shape(layers - 1, size // 2, size // 2),
-        shape(layers, size, LANES, dtype=F32),
+        shape(size, LANES, dtype=F32),
         shape(size, (variables + 2) * days),
         shape(days, size),
-        shape(n_block, LANES, LANES),
         shape(n_block, LANES, dtype=F32),
     )
     weights = pl.pallas_call(
         functools.partial(weights_kernel, width),
         out_shape=made,
         in_specs=[HBM] * 7,
-        out_specs=(HBM,) * 8,
+        out_specs=(HBM,) * 7,
         scratch_shapes=[pltpu.SMEM(params[0].shape, F32)]
         + [pltpu.VMEM(a.shape, a.dtype) for a in params[1:]]
         + [pltpu.VMEM(a.shape, a.dtype) for a in made]
@@ -526,24 +538,26 @@
     return pl.pallas_call(
         functools.partial(main_kernel, sources),
         out_shape=jax.ShapeDtypeStruct((days, rows, cols), F32),
-        in_specs=[VMEM] * 5 + [SMEM] + [HBM] * 8,
+        in_specs=[VMEM] * 4 + [SMEM] + [HBM] * 8,
         out_specs=VMEM,
         scratch_shapes=[
             pltpu.VMEM((n_block, channels * days, LANES), BF),
             pltpu.VMEM((n_block + 4, channels * days, LANES), BF),
             pltpu.VMEM((n_block, days, LANES), F32),
+            pltpu.VMEM((layers, size, LANES), F32),
+            pltpu.VMEM(arrived.shape, BF),
         ]
         + [pltpu.VMEM(a.shape, a.dtype) for a in made]
         + [pltpu.SemaphoreType.DMA((layers,)), pltpu.SemaphoreType.DMA((8,))],
         compiler_params=pltpu.CompilerParams(vmem_limit_bytes=60 * 2**20),
         name="blocks",
     )(
-        arrived,
         land,
         land_left,
         land_right,
         land_mask,
         out_bias,
+        arrived,
         *weights,
     )
 

time: 61 us -> 59.3 us (0.972)
  Pallas kernels: 36.4 us -> 34.7 us
    pallas_call x1, Pallas kernels: 22.8 us -> 21.7 us  [local(): pl.pallas_call(functools.partial(main_kernel, sources), out_shape=jax.Sha...]
  transfers between devices with their start and end apart: 5 -> 5, of which waited for: 1 -> 1; matrix products, arithmetic and copies ran while one was open for 1% -> 1% of each run, Pallas kernels for 16% -> 15%
where the time goes in v3:
time: 59.3 us; the launch traced here: 58.8 us
  Pallas kernels  34.7 us (59%)
  starting transfers between devices  18.2 us (31%)
  waiting for transfers between devices  3.33 us (6%)
  between operations  0.94 us (2%)
  local copies, waits for them, and re-layouts  0.91 us (2%)
  other arithmetic  0.71 us (1%)
    pallas_call x1, Pallas kernels, local(): pl.pallas_call(functools.partial(main_kernel, sources), out_shape=jax.Sha...  21.7 us
    pallas_call x1, Pallas kernels, local(): pl.pallas_call(functools.partial(weights_kernel, width), out_shape=made,...  9.01 us
    all_to_all x1, starting transfers between devices, local(): lax.all_to_all(outgoing, ('day', 'tile'), split_axis=0, concat_axis=0, ti...  6.22 us
    pallas_call x1, Pallas kernels, local(): pl.pallas_call(functools.partial(pack_kernel, tiles, bands, days_here), o...  4.01 us
    ppermute x1, starting transfers between devices, local(): land_right = lax.ppermute(land, 'tile', backward(tiles))  3.4 us
    ppermute x1, waiting for transfers between devices, local(): lax.ppermute(land[:HALO], 'day', backward(bands))  3.32 us
    ppermute x1, starting transfers between devices, local(): land_left = lax.ppermute(land, 'tile', forward(tiles))  3.28 us
    ppermute x1, starting transfers between devices, local(): lax.ppermute(land[rows - HALO:], 'day', forward(bands))  3.09 us
  transfers between devices with their start and end apart: 5, of which 1 were waited for; matrix products, arithmetic and copies ran while one was open for 1% of the time, Pallas kernels for 15%

profile of v3, /device:TPU:19, one launch (start us, length us, event | category | flops | bytes accessed | tf_op | source)
XLA Modules:
  0.0 58.8 jit_solution(3292192792909186598)
XLA Ops:
  0.0 4.0 %pack.1 = bf16[32,104,128]{2,1,0:T(8,128)(2,1)} custom-call(bf16[4,512,128]{2,1,0:T(8,128)(2,1)} %bitcast.9, s32[3,4,8]{2,1,0:T(4,128)} %bitcast.10), custom_call_target="tpu_custom_call" | custom-call | tf_op jit(solution)/shard_map/pack/pallas_call | solution.py:470
  4.0 6.2 %all-to-all-start = ((bf16[32,104,128]{2,1,0:T(8,128)(2,1)}), bf16[32,104,128]{2,1,0:T(8,128)(2,1)S(1)}, u32[]{:S(2)}, u32[]{:S(2)}) async-start(bf16[32,104,128]{2,1,0:T(8,128)(2,1)} %pack.1), calls=%async_computation | async-start | bytes 1703936 | tf_op jit(solution)/shard_map/all_to_all | solution.py:522
  10.3 0.7 %convert_element_type.3 = bf16[16,128]{1,0:T(8,128)(2,1)S(1)} convert(s32[16,128]{1,0:T(8,128)} %own_land_ref) | non-fusion elementwise | flops 2048 | bytes 12288 | tf_op jit(solution)/shard_map/convert_element_type | solution.py:526
  11.0 3.1 %collective-permute-start = (bf16[4,128]{1,0:T(4,128)(2,1)S(1)}, bf16[4,128]{1,0:T(4,128)(2,1)S(1)}, u32[]{:S(2)}, u32[]{:S(2)}) collective-permute-start(bf16[4,128]{1,0:T(4,128)(2,1)S(1)} %get-tuple-element.25), channel_id=1, source_target_pairs={{0,8},{8,16},{16,24},{1,9},{9,17},{17,25},{2,10},{10,18},{18,26},{... | collective-permute-start | bytes 3080 | tf_op jit(solution)/shard_map/ppermute | solution.py:529
  14.1 2.2 %collective-permute-start.1 = (bf16[4,128]{1,0:T(4,128)(2,1)S(1)}, bf16[4,128]{1,0:T(4,128)(2,1)S(1)}, u32[]{:S(2)}, u32[]{:S(2)}) collective-permute-start(bf16[4,128]{1,0:T(4,128)(2,1)S(1)} %get-tuple-element.26), channel_id=1, source_target_pairs={{8,0},{16,8},{24,16},{9,1},{17,9},{25,17},{10,2},{18,10},{26,18},{... | collective-permute-start | bytes 3080 | tf_op jit(solution)/shard_map/ppermute | solution.py:531
  16.2 0.0 collective-permute-done
  16.3 3.3 %collective-permute-done.1 = bf16[4,128]{1,0:T(4,128)(2,1)S(1)} collective-permute-done((bf16[4,128]{1,0:T(4,128)(2,1)S(1)}, bf16[4,128]{1,0:T(4,128)(2,1)S(1)}, u32[]{:S(2)}, u32[]{:S(2)}) %collective-permute-start.1) | collective-permute-done | bytes 1056 | tf_op jit(solution)/shard_map/ppermute | solution.py:531
  19.6 0.0 copy-start.1
  19.6 3.4 %collective-permute-start.3 = (bf16[24,128]{1,0:T(8,128)(2,1)S(1)}, bf16[24,128]{1,0:T(8,128)(2,1)S(1)}, u32[]{:S(2)}, u32[]{:S(2)}) collective-permute-start(bf16[24,128]{1,0:T(8,128)(2,1)S(1)} %pad_maximum_fusion.land_ref), channel_id=1, source_target_pairs={{1,0},{2,1},{3,2},{4,3},{5,4},{6,5},{7,6},{9,8},{10,9},{11,10},{12... | collective-permute-start | bytes 18440 | tf_op jit(solution)/shard_map/ppermute | solution.py:536
  23.0 3.3 %collective-permute-start.2 = (bf16[24,128]{1,0:T(8,128)(2,1)S(1)}, bf16[24,128]{1,0:T(8,128)(2,1)S(1)}, u32[]{:S(2)}, u32[]{:S(2)}) collective-permute-start(bf16[24,128]{1,0:T(8,128)(2,1)S(1)} %pad_maximum_fusion.land_ref), channel_id=1, source_target_pairs={{0,1},{1,2},{2,3},{3,4},{4,5},{5,6},{6,7},{8,9},{9,10},{10,11},{11... | collective-permute-start | bytes 18440 | tf_op jit(solution)/shard_map/ppermute | solution.py:535
  26.3 9.0 %weights.1 = (bf16[4,16,5,128,128]{4,3,2,1,0:T(8,128)(2,1)}, bf16[512,512]{1,0:T(8,128)(2,1)}, bf16[3,256,256]{2,1,0:T(8,128)(2,1)}, f32[512,128]{1,0:T(8,128)},...) custom-call(f32[9,4,16]{2,1,0:T(4,128)} %bitcast.11, f32[3,4,16]{2,1,0:T(4,128)} %bitcast.12, ...), custom_call_target="tpu_custom_call" | custom-call | flops 2000000000 | bytes 25165824 | tf_op jit(solution)/shard_map/weights/pallas_call | solution.py:509
  36.0 0.0 collective-permute-done.3.land_right_ref
  36.0 0.0 copy-start.2
  36.0 0.0 collective-permute-done.2.land_left_ref
  36.0 0.0 copy-start.3
  36.0 0.0 all-to-all-done.refs_0_
  36.0 0.0 copy-start
  36.0 0.0 copy-done.1
  36.0 0.5 copy-done.2
  36.6 0.0 copy-done.3
  36.6 0.3 copy-done
  36.9 21.7 %blocks.1 = f32[32,16,128]{2,1,0:T(8,128)} custom-call(bf16[24,128]{1,0:T(8,128)(2,1)} %copy-done.1, bf16[24,128]{1,0:T(8,128)(2,1)} %copy-done.3, bf16[24,128]{1,0:T(8,128)(2,1)} %copy-done.2, s32[16,128]{1,0:T(8,128)} %own_land_ref, f32[1]{0:T(128)S(6)} %copy.12.out_b_ref, bf16[32,104,128]{2,1,0:T(8,128)(2,1)} %copy-done, ...), custom_call_target="tpu_custom_call" | custom-call | tf_op jit(solution)/shard_map/blocks/pallas_call | solution.py:538
  (2 shorter events, 0.0 us)
Async XLA Ops:
  4.0 32.0 %all-to-all-start = ((bf16[32,104,128]{2,1,0:T(8,128)(2,1)}), bf16[32,104,128]{2,1,0:T(8,128)(2,1)S(1)}, u32[]{:S(2)}, u32[]{:S(2)}) async-start(bf16[32,104,128]{2,1,0:T(8,128)(2,1)} %pack.1), calls=%async_computation | async-start | bytes 1703936 | tf_op jit(solution)/shard_map/all_to_all | solution.py:522
  11.0 5.3 %collective-permute-start = (bf16[4,128]{1,0:T(4,128)(2,1)S(1)}, bf16[4,128]{1,0:T(4,128)(2,1)S(1)}, u32[]{:S(2)}, u32[]{:S(2)}) collective-permute-start(bf16[4,128]{1,0:T(4,128)(2,1)S(1)} %get-tuple-element.25), channel_id=1, source_target_pairs={{0,8},{8,16},{16,24},{1,9},{9,17},{17,25},{2,10},{10,18},{18,26},{... | collective-permute-start | bytes 3080 | tf_op jit(solution)/shard_map/ppermute | solution.py:529
  14.1 5.5 %collective-permute-start.1 = (bf16[4,128]{1,0:T(4,128)(2,1)S(1)}, bf16[4,128]{1,0:T(4,128)(2,1)S(1)}, u32[]{:S(2)}, u32[]{:S(2)}) collective-permute-start(bf16[4,128]{1,0:T(4,128)(2,1)S(1)} %get-tuple-element.26), channel_id=1, source_target_pairs={{8,0},{16,8},{24,16},{9,1},{17,9},{25,17},{10,2},{18,10},{26,18},{... | collective-permute-start | bytes 3080 | tf_op jit(solution)/shard_map/ppermute | solution.py:531
  19.6 16.4 %copy-start.1 = (bf16[24,128]{1,0:T(8,128)(2,1)}, bf16[24,128]{1,0:T(8,128)(2,1)S(1)}, u32[]{:S(2)}) copy-start(bf16[24,128]{1,0:T(8,128)(2,1)S(1)} %pad_maximum_fusion.land_ref) | copy-start | bytes 18436
  19.6 16.4 %collective-permute-start.3 = (bf16[24,128]{1,0:T(8,128)(2,1)S(1)}, bf16[24,128]{1,0:T(8,128)(2,1)S(1)}, u32[]{:S(2)}, u32[]{:S(2)}) collective-permute-start(bf16[24,128]{1,0:T(8,128)(2,1)S(1)} %pad_maximum_fusion.land_ref), channel_id=1, source_target_pairs={{1,0},{2,1},{3,2},{4,3},{5,4},{6,5},{7,6},{9,8},{10,9},{11,10},{12... | collective-permute-start | bytes 18440 | tf_op jit(solution)/shard_map/ppermute | solution.py:536
  23.0 13.0 %collective-permute-start.2 = (bf16[24,128]{1,0:T(8,128)(2,1)S(1)}, bf16[24,128]{1,0:T(8,128)(2,1)S(1)}, u32[]{:S(2)}, u32[]{:S(2)}) collective-permute-start(bf16[24,128]{1,0:T(8,128)(2,1)S(1)} %pad_maximum_fusion.land_ref), channel_id=1, source_target_pairs={{0,1},{1,2},{2,3},{3,4},{4,5},{5,6},{6,7},{8,9},{9,10},{10,11},{11... | collective-permute-start | bytes 18440 | tf_op jit(solution)/shard_map/ppermute | solution.py:535
  36.0 0.6 %copy-start.2 = (bf16[24,128]{1,0:T(8,128)(2,1)}, bf16[24,128]{1,0:T(8,128)(2,1)S(1)}, u32[]{:S(2)}) copy-start(bf16[24,128]{1,0:T(8,128)(2,1)S(1)} %collective-permute-done.3.land_right_ref) | copy-start | bytes 18436
  36.0 0.6 %copy-start.3 = (bf16[24,128]{1,0:T(8,128)(2,1)}, bf16[24,128]{1,0:T(8,128)(2,1)S(1)}, u32[]{:S(2)}) copy-start(bf16[24,128]{1,0:T(8,128)(2,1)S(1)} %collective-permute-done.2.land_left_ref) | copy-start | bytes 18436
  36.0 0.9 %copy-start = (bf16[32,104,128]{2,1,0:T(8,128)(2,1)}, bf16[32,104,128]{2,1,0:T(8,128)(2,1)S(1)}, u32[]{:S(2)}) copy-start(bf16[32,104,128]{2,1,0:T(8,128)(2,1)S(1)} %all-to-all-done.refs_0_) | copy-start | bytes 2555908

commit v4 on v3

--- a/solution.py
+++ b/solution.py
@@ -240,26 +240,23 @@
 
 def main_kernel(
     sources,
-    land_ref,
-    land_left_ref,
-    land_right_ref,
-    own_land_ref,
     out_b_ref,
     *refs,
 ):
-    given, out_ref, x_ref, v_ref, y_ref, bias_ref = refs[:8], refs[8], refs[9], refs[10], refs[11], refs[12]
-    held, taps_sem, sem = refs[13:21], refs[21], refs[22]
-    arrived_ref, banded_ref, first_ref, rest_ref, column_ref, in_ref, out_w_ref, valid_ref = held
-    names = ("arrived", "banded", "first", "rest", "column", "in", "out", "valid")
+    given, out_ref, x_ref, v_ref, y_ref, bias_ref = refs[:12], refs[12], refs[13], refs[14], refs[15], refs[16]
+    held, taps_sem, sem = refs[17:29], refs[29], refs[30]
+    names = ("arrived", "land", "left", "right", "own", "banded", "first", "rest", "column", "in", "out", "valid")
+    arrived_ref, land_ref, land_left_ref, land_right_ref, own_land_ref = held[:5]
+    banded_ref, first_ref, rest_ref, column_ref, in_ref, out_w_ref, valid_ref = held[5:]
     copies = {
         name: pltpu.make_async_copy(a, b, sem.at[i])
         for i, (name, a, b) in enumerate(zip(names, given, held))
         if name != "banded"
     }
-    for name in ("arrived", "in", "column", "first", "valid", "rest", "out"):
+    for name in ("arrived", "land", "left", "right", "in", "column", "first", "valid", "rest", "out", "own"):
         copies[name].start()
     fetch = [
-        pltpu.make_async_copy(given[1].at[l], banded_ref.at[l], taps_sem.at[l]) for l in range(banded_ref.shape[0])
+        pltpu.make_async_copy(given[5].at[l], banded_ref.at[l], taps_sem.at[l]) for l in range(banded_ref.shape[0])
     ]
     channels = banded_ref.shape[1]
     layers = banded_ref.shape[0]
@@ -340,6 +337,8 @@
         edge = edges[0] if b <= 16 else edges[1]
         return jnp.where(lane < start - 8, before_v, jnp.where(lane < start, edge, now_v))
 
+    for name in ("land", "left", "right"):
+        copies[name].wait()
     land, land_left, land_right = (
         pltpu.roll(
             jnp.concatenate([ref[...].astype(F32), jnp.zeros((LANES - rows_in, LANES), F32)], 0), 4, 1, stride=8, stride_axis=0
@@ -424,6 +423,7 @@
             stencil(l, pairs_x, c)
 
     copies["out"].wait()
+    copies["own"].wait()
     for j in range(2, 11):
         got = jnp.dot(
             out_w_ref[...], jnp.concatenate([x_ref[2 * j], x_ref[2 * j + 1]], 1), preferred_element_type=F32
@@ -538,28 +538,20 @@
     return pl.pallas_call(
         functools.partial(main_kernel, sources),
         out_shape=jax.ShapeDtypeStruct((days, rows, cols), F32),
-        in_specs=[VMEM] * 4 + [SMEM] + [HBM] * 8,
+        in_specs=[SMEM] + [HBM] * 12,
         out_specs=VMEM,
         scratch_shapes=[
             pltpu.VMEM((n_block, channels * days, LANES), BF),
             pltpu.VMEM((n_block + 4, channels * days, LANES), BF),
             pltpu.VMEM((n_block, days, LANES), F32),
             pltpu.VMEM((layers, size, LANES), F32),
-            pltpu.VMEM(arrived.shape, BF),
         ]
+        + [pltpu.VMEM(a.shape, a.dtype) for a in (arrived, land, land_left, land_right, land_mask)]
         + [pltpu.VMEM(a.shape, a.dtype) for a in made]
-        + [pltpu.SemaphoreType.DMA((layers,)), pltpu.SemaphoreType.DMA((8,))],
+        + [pltpu.SemaphoreType.DMA((layers,)), pltpu.SemaphoreType.DMA((12,))],
         compiler_params=pltpu.CompilerParams(vmem_limit_bytes=60 * 2**20),
         name="blocks",
-    )(
-        land,
-        land_left,
-        land_right,
-        land_mask,
-        out_bias,
-        arrived,
-        *weights,
-    )
+    )(out_bias, arrived, land, land_left, land_right, land_mask, *weights)
 
 
 def solution(mesh):

time: 59.3 us -> 58.7 us (0.990)
  Pallas kernels: 34.7 us -> 34.1 us
    pallas_call x1, Pallas kernels: 21.7 us -> 21.1 us  [local(): pl.pallas_call(functools.partial(main_kernel, sources), out_shape=jax.Sha...]
where the time goes in v4:
time: 58.7 us; the launch traced here: 58.2 us
  Pallas kernels  34.1 us (58%)
  starting transfers between devices  18.2 us (31%)
  waiting for transfers between devices  3.33 us (6%)
  between operations  0.94 us (2%)
  local copies, waits for them, and re-layouts  0.91 us (2%)
  other arithmetic  0.71 us (1%)
    pallas_call x1, Pallas kernels, local(): pl.pallas_call(functools.partial(main_kernel, sources), out_shape=jax.Sha...  21.1 us
    pallas_call x1, Pallas kernels, local(): pl.pallas_call(functools.partial(weights_kernel, width), out_shape=made,...  9.01 us
    all_to_all x1, starting transfers between devices, local(): lax.all_to_all(outgoing, ('day', 'tile'), split_axis=0, concat_axis=0, ti...  6.22 us
    pallas_call x1, Pallas kernels, local(): pl.pallas_call(functools.partial(pack_kernel, tiles, bands, days_here), o...  4.01 us
    ppermute x1, starting transfers between devices, local(): land_right = lax.ppermute(land, 'tile', backward(tiles))  3.4 us
    ppermute x1, waiting for transfers between devices, local(): lax.ppermute(land[:HALO], 'day', backward(bands))  3.32 us
    ppermute x1, starting transfers between devices, local(): land_left = lax.ppermute(land, 'tile', forward(tiles))  3.28 us
    ppermute x1, starting transfers between devices, local(): lax.ppermute(land[rows - HALO:], 'day', forward(bands))  3.09 us
  transfers between devices with their start and end apart: 5, of which 1 were waited for; matrix products, arithmetic and copies ran while one was open for 1% of the time, Pallas kernels for 15%

profile of v4, /device:TPU:19, one launch (start us, length us, event | category | flops | bytes accessed | tf_op | source)
XLA Modules:
  0.0 58.2 jit_solution(12869241206365530281)
XLA Ops:
  0.0 4.0 %pack.1 = bf16[32,104,128]{2,1,0:T(8,128)(2,1)} custom-call(bf16[4,512,128]{2,1,0:T(8,128)(2,1)} %bitcast.9, s32[3,4,8]{2,1,0:T(4,128)} %bitcast.10), custom_call_target="tpu_custom_call" | custom-call | tf_op jit(solution)/shard_map/pack/pallas_call | solution.py:470
  4.0 6.2 %all-to-all-start = ((bf16[32,104,128]{2,1,0:T(8,128)(2,1)}), bf16[32,104,128]{2,1,0:T(8,128)(2,1)S(1)}, u32[]{:S(2)}, u32[]{:S(2)}) async-start(bf16[32,104,128]{2,1,0:T(8,128)(2,1)} %pack.1), calls=%async_computation | async-start | bytes 1703936 | tf_op jit(solution)/shard_map/all_to_all | solution.py:522
  10.3 0.7 %convert_element_type.3 = bf16[16,128]{1,0:T(8,128)(2,1)S(1)} convert(s32[16,128]{1,0:T(8,128)} %refs_4_) | non-fusion elementwise | flops 2048 | bytes 12288 | tf_op jit(solution)/shard_map/convert_element_type | solution.py:526
  11.0 3.1 %collective-permute-start = (bf16[4,128]{1,0:T(4,128)(2,1)S(1)}, bf16[4,128]{1,0:T(4,128)(2,1)S(1)}, u32[]{:S(2)}, u32[]{:S(2)}) collective-permute-start(bf16[4,128]{1,0:T(4,128)(2,1)S(1)} %get-tuple-element.25), channel_id=1, source_target_pairs={{0,8},{8,16},{16,24},{1,9},{9,17},{17,25},{2,10},{10,18},{18,26},{... | collective-permute-start | bytes 3080 | tf_op jit(solution)/shard_map/ppermute | solution.py:529
  14.1 2.2 %collective-permute-start.1 = (bf16[4,128]{1,0:T(4,128)(2,1)S(1)}, bf16[4,128]{1,0:T(4,128)(2,1)S(1)}, u32[]{:S(2)}, u32[]{:S(2)}) collective-permute-start(bf16[4,128]{1,0:T(4,128)(2,1)S(1)} %get-tuple-element.26), channel_id=1, source_target_pairs={{8,0},{16,8},{24,16},{9,1},{17,9},{25,17},{10,2},{18,10},{26,18},{... | collective-permute-start | bytes 3080 | tf_op jit(solution)/shard_map/ppermute | solution.py:531
  16.2 0.0 collective-permute-done
  16.3 3.3 %collective-permute-done.1 = bf16[4,128]{1,0:T(4,128)(2,1)S(1)} collective-permute-done((bf16[4,128]{1,0:T(4,128)(2,1)S(1)}, bf16[4,128]{1,0:T(4,128)(2,1)S(1)}, u32[]{:S(2)}, u32[]{:S(2)}) %collective-permute-start.1) | collective-permute-done | bytes 1056 | tf_op jit(solution)/shard_map/ppermute | solution.py:531
  19.6 0.0 copy-start.1
  19.6 3.4 %collective-permute-start.3 = (bf16[24,128]{1,0:T(8,128)(2,1)S(1)}, bf16[24,128]{1,0:T(8,128)(2,1)S(1)}, u32[]{:S(2)}, u32[]{:S(2)}) collective-permute-start(bf16[24,128]{1,0:T(8,128)(2,1)S(1)} %pad_maximum_fusion.refs_1_), channel_id=1, source_target_pairs={{1,0},{2,1},{3,2},{4,3},{5,4},{6,5},{7,6},{9,8},{10,9},{11,10},{12... | collective-permute-start | bytes 18440 | tf_op jit(solution)/shard_map/ppermute | solution.py:536
  23.0 3.3 %collective-permute-start.2 = (bf16[24,128]{1,0:T(8,128)(2,1)S(1)}, bf16[24,128]{1,0:T(8,128)(2,1)S(1)}, u32[]{:S(2)}, u32[]{:S(2)}) collective-permute-start(bf16[24,128]{1,0:T(8,128)(2,1)S(1)} %pad_maximum_fusion.refs_1_), channel_id=1, source_target_pairs={{0,1},{1,2},{2,3},{3,4},{4,5},{5,6},{6,7},{8,9},{9,10},{10,11},{11... | collective-permute-start | bytes 18440 | tf_op jit(solution)/shard_map/ppermute | solution.py:535
  26.3 9.0 %weights.1 = (bf16[4,16,5,128,128]{4,3,2,1,0:T(8,128)(2,1)}, bf16[512,512]{1,0:T(8,128)(2,1)}, bf16[3,256,256]{2,1,0:T(8,128)(2,1)}, f32[512,128]{1,0:T(8,128)},...) custom-call(f32[9,4,16]{2,1,0:T(4,128)} %bitcast.11, f32[3,4,16]{2,1,0:T(4,128)} %bitcast.12, ...), custom_call_target="tpu_custom_call" | custom-call | flops 2000000000 | bytes 25165824 | tf_op jit(solution)/shard_map/weights/pallas_call | solution.py:509
  36.0 0.0 collective-permute-done.3.refs_3_
  36.0 0.0 copy-start.2
  36.0 0.0 collective-permute-done.2.refs_2_
  36.0 0.0 copy-start.3
  36.0 0.0 all-to-all-done.refs_0_
  36.0 0.0 copy-start
  36.0 0.0 copy-done.1
  36.0 0.5 copy-done.2
  36.6 0.0 copy-done.3
  36.6 0.3 copy-done
  36.9 21.1 %blocks.1 = f32[32,16,128]{2,1,0:T(8,128)} custom-call(f32[1]{0:T(128)S(6)} %copy.12.out_b_ref, bf16[32,104,128]{2,1,0:T(8,128)(2,1)} %copy-done, bf16[24,128]{1,0:T(8,128)(2,1)} %copy-done.1, bf16[24,128]{1,0:T(8,128)(2,1)} %copy-done.3, bf16[24,128]{1,0:T(8,128)(2,1)} %copy-done.2, s32[16,128]{1,0:T(8,128)} %refs_4_, ...), custom_call_target="tpu_custom_call" | custom-call | tf_op jit(solution)/shard_map/blocks/pallas_call | solution.py:538
  (2 shorter events, 0.0 us)
Async XLA Ops:
  4.0 32.0 %all-to-all-start = ((bf16[32,104,128]{2,1,0:T(8,128)(2,1)}), bf16[32,104,128]{2,1,0:T(8,128)(2,1)S(1)}, u32[]{:S(2)}, u32[]{:S(2)}) async-start(bf16[32,104,128]{2,1,0:T(8,128)(2,1)} %pack.1), calls=%async_computation | async-start | bytes 1703936 | tf_op jit(solution)/shard_map/all_to_all | solution.py:522
  11.0 5.3 %collective-permute-start = (bf16[4,128]{1,0:T(4,128)(2,1)S(1)}, bf16[4,128]{1,0:T(4,128)(2,1)S(1)}, u32[]{:S(2)}, u32[]{:S(2)}) collective-permute-start(bf16[4,128]{1,0:T(4,128)(2,1)S(1)} %get-tuple-element.25), channel_id=1, source_target_pairs={{0,8},{8,16},{16,24},{1,9},{9,17},{17,25},{2,10},{10,18},{18,26},{... | collective-permute-start | bytes 3080 | tf_op jit(solution)/shard_map/ppermute | solution.py:529
  14.1 5.5 %collective-permute-start.1 = (bf16[4,128]{1,0:T(4,128)(2,1)S(1)}, bf16[4,128]{1,0:T(4,128)(2,1)S(1)}, u32[]{:S(2)}, u32[]{:S(2)}) collective-permute-start(bf16[4,128]{1,0:T(4,128)(2,1)S(1)} %get-tuple-element.26), channel_id=1, source_target_pairs={{8,0},{16,8},{24,16},{9,1},{17,9},{25,17},{10,2},{18,10},{26,18},{... | collective-permute-start | bytes 3080 | tf_op jit(solution)/shard_map/ppermute | solution.py:531
  19.6 16.4 %copy-start.1 = (bf16[24,128]{1,0:T(8,128)(2,1)}, bf16[24,128]{1,0:T(8,128)(2,1)S(1)}, u32[]{:S(2)}) copy-start(bf16[24,128]{1,0:T(8,128)(2,1)S(1)} %pad_maximum_fusion.refs_1_) | copy-start | bytes 18436
  19.6 16.4 %collective-permute-start.3 = (bf16[24,128]{1,0:T(8,128)(2,1)S(1)}, bf16[24,128]{1,0:T(8,128)(2,1)S(1)}, u32[]{:S(2)}, u32[]{:S(2)}) collective-permute-start(bf16[24,128]{1,0:T(8,128)(2,1)S(1)} %pad_maximum_fusion.refs_1_), channel_id=1, source_target_pairs={{1,0},{2,1},{3,2},{4,3},{5,4},{6,5},{7,6},{9,8},{10,9},{11,10},{12... | collective-permute-start | bytes 18440 | tf_op jit(solution)/shard_map/ppermute | solution.py:536
  23.0 13.0 %collective-permute-start.2 = (bf16[24,128]{1,0:T(8,128)(2,1)S(1)}, bf16[24,128]{1,0:T(8,128)(2,1)S(1)}, u32[]{:S(2)}, u32[]{:S(2)}) collective-permute-start(bf16[24,128]{1,0:T(8,128)(2,1)S(1)} %pad_maximum_fusion.refs_1_), channel_id=1, source_target_pairs={{0,1},{1,2},{2,3},{3,4},{4,5},{5,6},{6,7},{8,9},{9,10},{10,11},{11... | collective-permute-start | bytes 18440 | tf_op jit(solution)/shard_map/ppermute | solution.py:535
  36.0 0.6 %copy-start.2 = (bf16[24,128]{1,0:T(8,128)(2,1)}, bf16[24,128]{1,0:T(8,128)(2,1)S(1)}, u32[]{:S(2)}) copy-start(bf16[24,128]{1,0:T(8,128)(2,1)S(1)} %collective-permute-done.3.refs_3_) | copy-start | bytes 18436
  36.0 0.6 %copy-start.3 = (bf16[24,128]{1,0:T(8,128)(2,1)}, bf16[24,128]{1,0:T(8,128)(2,1)S(1)}, u32[]{:S(2)}) copy-start(bf16[24,128]{1,0:T(8,128)(2,1)S(1)} %collective-permute-done.2.refs_2_) | copy-start | bytes 18436
  36.0 0.9 %copy-start = (bf16[32,104,128]{2,1,0:T(8,128)(2,1)}, bf16[32,104,128]{2,1,0:T(8,128)(2,1)S(1)}, u32[]{:S(2)}) copy-start(bf16[32,104,128]{2,1,0:T(8,128)(2,1)S(1)} %all-to-all-done.refs_0_) | copy-start | bytes 2555908

commit v5 on v4

--- a/solution.py
+++ b/solution.py
@@ -51,7 +51,7 @@
             for v in range(variables):
                 rows = wide[v, pl.ds(16 + first - offset, 16), :]
                 mixed[band, pl.ds(v, 16, stride=4), :] = jnp.where(live, rows, 0.0)
-            block = mixed[band].astype(BF)
+            block = mixed[band, 0:64].astype(BF)
             blocks[day * bands + band] = block
             out_ref[band * tiles + tile, 16:80] = block
             if band + 1 < bands:
@@ -475,7 +475,7 @@
         scratch_shapes=[
             pltpu.VMEM((variables, slots, cols), BF),
             pltpu.VMEM((variables, slots + 32, cols), F32),
-            pltpu.VMEM((bands, 64, cols), F32),
+            pltpu.VMEM((bands, 72, cols), F32),
             pltpu.VMEM((granules, 64, cols), BF),
             pltpu.VMEM((granules, 8, cols), F32),
             pltpu.VMEM(((bands + 2) * (tiles + 2), 8, cols), F32),

time: 58.7 us -> 58.7 us (level)
  no operation moved by 1% of the time
where the time goes in v5:
time: 58.7 us; the launch traced here: 58.2 us
  Pallas kernels  34.1 us (58%)
  starting transfers between devices  18.2 us (31%)
  waiting for transfers between devices  3.33 us (6%)
  between operations  0.94 us (2%)
  local copies, waits for them, and re-layouts  0.91 us (2%)
  other arithmetic  0.71 us (1%)
    pallas_call x1, Pallas kernels, local(): pl.pallas_call(functools.partial(main_kernel, sources), out_shape=jax.Sha...  21.1 us
    pallas_call x1, Pallas kernels, local(): pl.pallas_call(functools.partial(weights_kernel, width), out_shape=made,...  9.01 us
    all_to_all x1, starting transfers between devices, local(): lax.all_to_all(outgoing, ('day', 'tile'), split_axis=0, concat_axis=0, ti...  6.24 us
    pallas_call x1, Pallas kernels, local(): pl.pallas_call(functools.partial(pack_kernel, tiles, bands, days_here), o...  4.01 us
    ppermute x1, starting transfers between devices, local(): land_right = lax.ppermute(land, 'tile', backward(tiles))  3.4 us
    ppermute x1, waiting for transfers between devices, local(): lax.ppermute(land[:HALO], 'day', backward(bands))  3.32 us
    ppermute x1, starting transfers between devices, local(): land_left = lax.ppermute(land, 'tile', forward(tiles))  3.28 us
    ppermute x1, starting transfers between devices, local(): lax.ppermute(land[rows - HALO:], 'day', forward(bands))  3.09 us
  transfers between devices with their start and end apart: 5, of which 1 were waited for; matrix products, arithmetic and copies ran while one was open for 1% of the time, Pallas kernels for 15%

profile of v5, /device:TPU:19, one launch (start us, length us, event | category | flops | bytes accessed | tf_op | source)
XLA Modules:
  0.0 58.2 jit_solution(14868457696466888352)
XLA Ops:
  0.0 4.0 %pack.1 = bf16[32,104,128]{2,1,0:T(8,128)(2,1)} custom-call(bf16[4,512,128]{2,1,0:T(8,128)(2,1)} %bitcast.9, s32[3,4,8]{2,1,0:T(4,128)} %bitcast.10), custom_call_target="tpu_custom_call" | custom-call | tf_op jit(solution)/shard_map/pack/pallas_call | solution.py:470
  4.0 6.2 %all-to-all-start = ((bf16[32,104,128]{2,1,0:T(8,128)(2,1)}), bf16[32,104,128]{2,1,0:T(8,128)(2,1)S(1)}, u32[]{:S(2)}, u32[]{:S(2)}) async-start(bf16[32,104,128]{2,1,0:T(8,128)(2,1)} %pack.1), calls=%async_computation | async-start | bytes 1703936 | tf_op jit(solution)/shard_map/all_to_all | solution.py:522
  10.3 0.7 %convert_element_type.3 = bf16[16,128]{1,0:T(8,128)(2,1)S(1)} convert(s32[16,128]{1,0:T(8,128)} %refs_4_) | non-fusion elementwise | flops 2048 | bytes 12288 | tf_op jit(solution)/shard_map/convert_element_type | solution.py:526
  11.0 3.1 %collective-permute-start = (bf16[4,128]{1,0:T(4,128)(2,1)S(1)}, bf16[4,128]{1,0:T(4,128)(2,1)S(1)}, u32[]{:S(2)}, u32[]{:S(2)}) collective-permute-start(bf16[4,128]{1,0:T(4,128)(2,1)S(1)} %get-tuple-element.25), channel_id=1, source_target_pairs={{0,8},{8,16},{16,24},{1,9},{9,17},{17,25},{2,10},{10,18},{18,26},{... | collective-permute-start | bytes 3080 | tf_op jit(solution)/shard_map/ppermute | solution.py:529
  14.1 2.2 %collective-permute-start.1 = (bf16[4,128]{1,0:T(4,128)(2,1)S(1)}, bf16[4,128]{1,0:T(4,128)(2,1)S(1)}, u32[]{:S(2)}, u32[]{:S(2)}) collective-permute-start(bf16[4,128]{1,0:T(4,128)(2,1)S(1)} %get-tuple-element.26), channel_id=1, source_target_pairs={{8,0},{16,8},{24,16},{9,1},{17,9},{25,17},{10,2},{18,10},{26,18},{... | collective-permute-start | bytes 3080 | tf_op jit(solution)/shard_map/ppermute | solution.py:531
  16.3 0.0 collective-permute-done
  16.3 3.3 %collective-permute-done.1 = bf16[4,128]{1,0:T(4,128)(2,1)S(1)} collective-permute-done((bf16[4,128]{1,0:T(4,128)(2,1)S(1)}, bf16[4,128]{1,0:T(4,128)(2,1)S(1)}, u32[]{:S(2)}, u32[]{:S(2)}) %collective-permute-start.1) | collective-permute-done | bytes 1056 | tf_op jit(solution)/shard_map/ppermute | solution.py:531
  19.6 0.0 copy-start.1
  19.6 3.4 %collective-permute-start.3 = (bf16[24,128]{1,0:T(8,128)(2,1)S(1)}, bf16[24,128]{1,0:T(8,128)(2,1)S(1)}, u32[]{:S(2)}, u32[]{:S(2)}) collective-permute-start(bf16[24,128]{1,0:T(8,128)(2,1)S(1)} %pad_maximum_fusion.refs_1_), channel_id=1, source_target_pairs={{1,0},{2,1},{3,2},{4,3},{5,4},{6,5},{7,6},{9,8},{10,9},{11,10},{12... | collective-permute-start | bytes 18440 | tf_op jit(solution)/shard_map/ppermute | solution.py:536
  23.0 3.3 %collective-permute-start.2 = (bf16[24,128]{1,0:T(8,128)(2,1)S(1)}, bf16[24,128]{1,0:T(8,128)(2,1)S(1)}, u32[]{:S(2)}, u32[]{:S(2)}) collective-permute-start(bf16[24,128]{1,0:T(8,128)(2,1)S(1)} %pad_maximum_fusion.refs_1_), channel_id=1, source_target_pairs={{0,1},{1,2},{2,3},{3,4},{4,5},{5,6},{6,7},{8,9},{9,10},{10,11},{11... | collective-permute-start | bytes 18440 | tf_op jit(solution)/shard_map/ppermute | solution.py:535
  26.3 9.0 %weights.1 = (bf16[4,16,5,128,128]{4,3,2,1,0:T(8,128)(2,1)}, bf16[512,512]{1,0:T(8,128)(2,1)}, bf16[3,256,256]{2,1,0:T(8,128)(2,1)}, f32[512,128]{1,0:T(8,128)},...) custom-call(f32[9,4,16]{2,1,0:T(4,128)} %bitcast.11, f32[3,4,16]{2,1,0:T(4,128)} %bitcast.12, ...), custom_call_target="tpu_custom_call" | custom-call | flops 2000000000 | bytes 25165824 | tf_op jit(solution)/shard_map/weights/pallas_call | solution.py:509
  36.0 0.0 collective-permute-done.3.refs_3_
  36.0 0.0 copy-start.2
  36.0 0.0 collective-permute-done.2.refs_2_
  36.0 0.0 copy-start.3
  36.0 0.0 all-to-all-done.refs_0_
  36.0 0.0 copy-start
  36.0 0.0 copy-done.1
  36.0 0.5 copy-done.2
  36.6 0.0 copy-done.3
  36.6 0.3 copy-done
  36.9 21.1 %blocks.1 = f32[32,16,128]{2,1,0:T(8,128)} custom-call(f32[1]{0:T(128)S(6)} %copy.12.out_b_ref, bf16[32,104,128]{2,1,0:T(8,128)(2,1)} %copy-done, bf16[24,128]{1,0:T(8,128)(2,1)} %copy-done.1, bf16[24,128]{1,0:T(8,128)(2,1)} %copy-done.3, bf16[24,128]{1,0:T(8,128)(2,1)} %copy-done.2, s32[16,128]{1,0:T(8,128)} %refs_4_, ...), custom_call_target="tpu_custom_call" | custom-call | tf_op jit(solution)/shard_map/blocks/pallas_call | solution.py:538
  (2 shorter events, 0.0 us)
Async XLA Ops:
  4.0 32.0 %all-to-all-start = ((bf16[32,104,128]{2,1,0:T(8,128)(2,1)}), bf16[32,104,128]{2,1,0:T(8,128)(2,1)S(1)}, u32[]{:S(2)}, u32[]{:S(2)}) async-start(bf16[32,104,128]{2,1,0:T(8,128)(2,1)} %pack.1), calls=%async_computation | async-start | bytes 1703936 | tf_op jit(solution)/shard_map/all_to_all | solution.py:522
  11.0 5.3 %collective-permute-start = (bf16[4,128]{1,0:T(4,128)(2,1)S(1)}, bf16[4,128]{1,0:T(4,128)(2,1)S(1)}, u32[]{:S(2)}, u32[]{:S(2)}) collective-permute-start(bf16[4,128]{1,0:T(4,128)(2,1)S(1)} %get-tuple-element.25), channel_id=1, source_target_pairs={{0,8},{8,16},{16,24},{1,9},{9,17},{17,25},{2,10},{10,18},{18,26},{... | collective-permute-start | bytes 3080 | tf_op jit(solution)/shard_map/ppermute | solution.py:529
  14.1 5.5 %collective-permute-start.1 = (bf16[4,128]{1,0:T(4,128)(2,1)S(1)}, bf16[4,128]{1,0:T(4,128)(2,1)S(1)}, u32[]{:S(2)}, u32[]{:S(2)}) collective-permute-start(bf16[4,128]{1,0:T(4,128)(2,1)S(1)} %get-tuple-element.26), channel_id=1, source_target_pairs={{8,0},{16,8},{24,16},{9,1},{17,9},{25,17},{10,2},{18,10},{26,18},{... | collective-permute-start | bytes 3080 | tf_op jit(solution)/shard_map/ppermute | solution.py:531
  19.6 16.4 %copy-start.1 = (bf16[24,128]{1,0:T(8,128)(2,1)}, bf16[24,128]{1,0:T(8,128)(2,1)S(1)}, u32[]{:S(2)}) copy-start(bf16[24,128]{1,0:T(8,128)(2,1)S(1)} %pad_maximum_fusion.refs_1_) | copy-start | bytes 18436
  19.6 16.4 %collective-permute-start.3 = (bf16[24,128]{1,0:T(8,128)(2,1)S(1)}, bf16[24,128]{1,0:T(8,128)(2,1)S(1)}, u32[]{:S(2)}, u32[]{:S(2)}) collective-permute-start(bf16[24,128]{1,0:T(8,128)(2,1)S(1)} %pad_maximum_fusion.refs_1_), channel_id=1, source_target_pairs={{1,0},{2,1},{3,2},{4,3},{5,4},{6,5},{7,6},{9,8},{10,9},{11,10},{12... | collective-permute-start | bytes 18440 | tf_op jit(solution)/shard_map/ppermute | solution.py:536
  23.0 13.0 %collective-permute-start.2 = (bf16[24,128]{1,0:T(8,128)(2,1)S(1)}, bf16[24,128]{1,0:T(8,128)(2,1)S(1)}, u32[]{:S(2)}, u32[]{:S(2)}) collective-permute-start(bf16[24,128]{1,0:T(8,128)(2,1)S(1)} %pad_maximum_fusion.refs_1_), channel_id=1, source_target_pairs={{0,1},{1,2},{2,3},{3,4},{4,5},{5,6},{6,7},{8,9},{9,10},{10,11},{11... | collective-permute-start | bytes 18440 | tf_op jit(solution)/shard_map/ppermute | solution.py:535
  36.0 0.6 %copy-start.2 = (bf16[24,128]{1,0:T(8,128)(2,1)}, bf16[24,128]{1,0:T(8,128)(2,1)S(1)}, u32[]{:S(2)}) copy-start(bf16[24,128]{1,0:T(8,128)(2,1)S(1)} %collective-permute-done.3.refs_3_) | copy-start | bytes 18436
  36.0 0.6 %copy-start.3 = (bf16[24,128]{1,0:T(8,128)(2,1)}, bf16[24,128]{1,0:T(8,128)(2,1)S(1)}, u32[]{:S(2)}) copy-start(bf16[24,128]{1,0:T(8,128)(2,1)S(1)} %collective-permute-done.2.refs_2_) | copy-start | bytes 18436
  36.0 0.9 %copy-start = (bf16[32,104,128]{2,1,0:T(8,128)(2,1)}, bf16[32,104,128]{2,1,0:T(8,128)(2,1)S(1)}, u32[]{:S(2)}) copy-start(bf16[32,104,128]{2,1,0:T(8,128)(2,1)S(1)} %all-to-all-done.refs_0_) | copy-start | bytes 2555908
